TPU v7x, 32 devices: a whole 2x2x4 slice. The times are simulated.
32 devices in a mesh: ctx: 8 (over y, x, core), tp: 4 (over z).
Axes of the slice: x: 2, y: 2, z: 4, core: 2. Of those that a mesh axis runs over, the one named last changes fastest.
Arguments:
- qkv_first: bfloat16 [3, 8192, 4096], P(None, 'ctx', 'tp'), may hold values from -6 to 6
- short_first: float32 [3, 3, 4096], P(None, None, 'tp'), may hold values from -4 to 4
- medium_filter: bfloat16 [4096, 128], P('tp'), may hold values from -0.5 to 0.5
- out_weight: bfloat16 [4096, 4096], P('tp', 'ctx'), may hold values from -0.09375 to 0.09375
- residual_in: bfloat16 [8192, 4096], P('ctx', 'tp'), may hold values from -64 to 64
- norm_gain: bfloat16 [4096], P('tp'), may hold values from 0.5 to 1.5
- in_weight: bfloat16 [3, 4096, 4096], P(None, 'ctx', 'tp'), may hold values from -0.09375 to 0.09375
- short_second: float32 [3, 3, 4096], P(None, None, 'tp'), may hold values from -4 to 4
- rates: float32 [16, 4096], P(None, 'tp'), as said below
- residues: float32 [16, 4096], P(None, 'tp'), may hold values from -0.024 to 0.024
- skip_gain: float32 [4096], P('tp'), may hold values from -4 to 4
Outputs:
- hidden: bfloat16 [8192, 4096], P('ctx', 'tp')
- mixed: bfloat16 [8192, 4096], P('ctx', 'tp')
Inputs may be any that keep to these rules, and one draw needn't show every extreme that they name: `rates`: each entry is a positive decay rate per token, between 1e-7 and 0.05.
All inputs are finite; a program needn't handle non-finite values.
Results may differ from a plain program's by a relative error of at most 0.025.
Values may be sent and summed in bfloat16 or wider, within the bound.
A program may use at most 128 MiB of HBM per device.

v0:
```python
import jax
import jax.numpy as jnp
from jax import lax
from jax.sharding import PartitionSpec as P

D = 4096


EPSILON = 1e-05


def shifted(x, axis, by):
    size = lax.axis_size(axis)
    pairs = [(i, i + by) for i in range(size) if 0 <= i + by < size]
    return lax.ppermute(x, axis, pairs)


def entering(x, axis, join, neutral):
    place = lax.axis_index(axis)
    gathered = jax.tree.map(
        lambda a, kind: lax.all_gather(a.astype(kind), axis), x, (jnp.bfloat16, jnp.bfloat16)
    )
    state = jax.tree.map(lambda a, e: jnp.zeros_like(a) + jnp.asarray(e, a.dtype), x, neutral)

    def one(lap, state):
        return join(
            state,
            jax.tree.map(
                lambda a, own: lax.dynamic_index_in_dim(a, lap, 0, False).astype(own.dtype),
                gathered,
                x,
            ),
        )

    return lax.fori_loop(0, place, one, state)


def featurize(extended, tap_weights):
    widened = extended.astype(jnp.float32)
    return (
        tap_weights[:, 0][:, None, :] * widened[:, 2:]
        + tap_weights[:, 1][:, None, :] * widened[:, 1:-1]
        + tap_weights[:, 2][:, None, :] * widened[:, :-2]
    )


def toeplitz_pair(filters):
    tap_count = filters.shape[1]
    padded = jnp.concatenate([filters, jnp.zeros_like(filters)], axis=1)
    row_index = lax.broadcasted_iota(jnp.int32, (tap_count, tap_count), 0)
    col_index = lax.broadcasted_iota(jnp.int32, (tap_count, tap_count), 1)
    nearby = padded[:, (row_index - col_index) % (2 * tap_count)]
    earlier = padded[:, row_index - col_index + tap_count]
    return (nearby, earlier)


def medium_conv(extended, filters):
    tap_count = filters.shape[1]
    length = extended.shape[0] - tap_count
    channels = extended.shape[1]
    group_size = min(channels, 128)
    block_count = length // tap_count
    current_rows = extended[tap_count:].reshape(block_count, tap_count, channels)
    previous_rows = extended[:length].reshape(block_count, tap_count, channels)

    def medium_one_group(group_index):
        lower = group_index * group_size
        nearby, earlier = toeplitz_pair(lax.dynamic_slice_in_dim(filters, lower, group_size, 0))
        current_part = lax.dynamic_slice_in_dim(current_rows, lower, group_size, 2)
        previous_part = lax.dynamic_slice_in_dim(previous_rows, lower, group_size, 2)
        return jnp.einsum(
            "gij,bjg->big", nearby, current_part, preferred_element_type=jnp.float32
        ) + jnp.einsum("gij,bjg->big", earlier, previous_part, preferred_element_type=jnp.float32)

    pieces = lax.map(medium_one_group, jnp.arange(channels // group_size, dtype=jnp.int32))
    return pieces.transpose(1, 2, 0, 3).reshape(length, channels)


def modal_prefix(inputs, rates, tap_count):
    length, channels = inputs.shape
    block_count = length // tap_count
    shaped = inputs.reshape(block_count, tap_count, channels)
    lag_steps = jnp.arange(tap_count, dtype=jnp.float32)
    to_end = jnp.exp(-rates[:, None, :] * (tap_count - 1 - lag_steps)[None, :, None])
    block_ends = jnp.einsum("njc,bjc->bnc", to_end, shaped, precision=lax.Precision.HIGHEST)
    block_decay = jnp.exp(-rates * tap_count)

    def advance(state, end_state):
        return (block_decay * state + end_state, state)

    local_end, starts = lax.scan(advance, jnp.zeros_like(rates), block_ends)
    return (shaped, starts, local_end)


def modal_finish(shaped, starts, state_in, rates, residues):
    block_count, tap_count, channels = shaped.shape
    block_steps = jnp.arange(block_count, dtype=jnp.float32) * tap_count
    starts = starts + jnp.exp(-rates[None] * block_steps[:, None, None]) * state_in[None]
    lag_steps = jnp.arange(tap_count, dtype=jnp.float32)
    entry_weights = residues[:, None, :] * jnp.exp(
        -rates[:, None, :] * (lag_steps + 1.0)[None, :, None]
    )
    crossing = jnp.einsum("nic,bnc->bic", entry_weights, starts, precision=lax.Precision.HIGHEST)
    kernel = jnp.sum(
        residues[:, None, :] * jnp.exp(-rates[:, None, :] * lag_steps[None, :, None]), axis=0
    )
    row_index = lax.broadcasted_iota(jnp.int32, (tap_count, tap_count), 0)
    col_index = lax.broadcasted_iota(jnp.int32, (tap_count, tap_count), 1)
    group_size = min(channels, 128)

    def modal_one_group(group_index):
        lower = group_index * group_size
        kernel_part = lax.dynamic_slice_in_dim(kernel, lower, group_size, 1)
        lower_kernel = jnp.where(
            (row_index >= col_index)[:, :, None],
            kernel_part[jnp.maximum(row_index - col_index, 0)],
            0.0,
        )
        input_part = lax.dynamic_slice_in_dim(shaped, lower, group_size, 2)
        return jnp.einsum("ijg,bjg->big", lower_kernel, input_part, precision=lax.Precision.HIGHEST)

    pieces = lax.map(modal_one_group, jnp.arange(channels // group_size, dtype=jnp.int32))
    inside = pieces.transpose(1, 2, 0, 3).reshape(block_count, tap_count, channels)
    return (crossing + inside).reshape(block_count * tap_count, channels)


def combine_states(earlier, later):
    return (earlier[0] * later[1] + later[0], earlier[1] * later[1])


def on_device(
    qkv_first,
    short_first,
    medium_filter,
    out_weight,
    residual_in,
    norm_gain,
    in_weight,
    short_second,
    rates,
    residues,
    skip_gain,
):
    length = qkv_first.shape[1]
    channels = qkv_first.shape[2]
    tap_count = medium_filter.shape[1]
    nothing = jnp.zeros((1, channels), jnp.bfloat16)
    upper_rim = shifted(qkv_first[:, length - 2 :], "ctx", 1)
    features = featurize(jnp.concatenate([upper_rim, qkv_first], axis=1), short_first)
    gated = (features[1] * features[2]).astype(jnp.bfloat16)
    rim_rows = shifted(gated[length - tap_count + 1 :], "ctx", 1)
    extended = jnp.concatenate([nothing, rim_rows, gated], axis=0)
    query = features[0]
    mixed_first = (query * medium_conv(extended, medium_filter)).astype(jnp.bfloat16)
    partial_value = jnp.dot(
        mixed_first,
        lax.all_gather(out_weight, "ctx", axis=1, tiled=True),
        preferred_element_type=jnp.float32,
    )
    summed_all = lax.psum(partial_value.astype(jnp.bfloat16), "tp").astype(jnp.float32)
    residual_all, gain_all = (
        lax.all_gather(residual_in, "tp", axis=1, tiled=True),
        lax.all_gather(norm_gain, "tp", axis=0, tiled=True),
    )
    hidden_all = (residual_all.astype(jnp.float32) + summed_all).astype(jnp.bfloat16)
    hidden_values = hidden_all.astype(jnp.float32)
    squares = jnp.sum(hidden_values * hidden_values, axis=1)
    inverse_rms = lax.rsqrt(squares / D + EPSILON)
    normed = (hidden_values * inverse_rms[:, None] * gain_all.astype(jnp.float32)).astype(
        jnp.bfloat16
    )
    hidden = lax.dynamic_slice_in_dim(hidden_all, lax.axis_index("tp") * channels, channels, 1)
    projected = jnp.einsum(
        "tr,krc->ktc",
        normed,
        lax.all_gather(in_weight, "ctx", axis=1, tiled=True),
        preferred_element_type=jnp.float32,
    )
    qkv_second = projected.astype(jnp.bfloat16)
    second_edge = shifted(qkv_second[:, length - 2 :], "ctx", 1)
    features_second = featurize(jnp.concatenate([second_edge, qkv_second], axis=1), short_second)
    gated_second = (features_second[1] * features_second[2]).astype(jnp.bfloat16)
    gated_values = gated_second.astype(jnp.float32)
    shaped, starts, local_end = modal_prefix(gated_values, rates, tap_count)
    device_decay = jnp.exp(-rates * length)
    state_in, _ = entering(
        (local_end, device_decay),
        "ctx",
        combine_states,
        (jnp.zeros_like(rates), jnp.ones_like(rates)),
    )
    modal = modal_finish(shaped, starts, state_in, rates, residues)
    mixed = (features_second[0] * (modal + skip_gain * gated_values)).astype(jnp.bfloat16)
    return (hidden, mixed)


def solution(mesh):
    placed = (
        P(None, "ctx", "tp"),
        P(None, None, "tp"),
        P("tp", None),
        P("tp", "ctx"),
        P("ctx", "tp"),
        P("tp"),
        P(None, "ctx", "tp"),
        P(None, None, "tp"),
        P(None, "tp"),
        P(None, "tp"),
        P("tp"),
    )
    return jax.shard_map(
        on_device,
        mesh=mesh,
        in_specs=placed,
        out_specs=(P("ctx", "tp"), P("ctx", "tp")),
        check_vma=False,
    )
```

profile of v0, /device:TPU:0, one launch (start us, length us, event | category | flops | bytes accessed | tf_op | source)
XLA Modules:
  0.0 2405.7 jit_solution(15572123936255013974)
XLA Ops:
  50.0 1132.5 %while.50 = (s32[]{:T(128)}, f32[8,8,128,128]{2,1,3,0:T(8,128)}, s32[8]{0:T(128)S(1)}, bf16[8,128,1024]{2,1,0:T(8,128)(2,1)}, bf16[1024,128]{1,0:T(8,128)(2,1)},...) while((s32[]{:T(128)}, f32[8,8,128,128]{2,1,3,0:T(8,128)}, ...), condition=%wide.region_1.2_spmd, body=%wide.region_0.1_spmd.sunk | while | flops 67600384 | bytes 46629052 | solution.py:75
  53.4 57.4 %gather_fusion = bf16[16384,128]{1,0:T(8,128)(2,1)} fusion(bf16[128,256]{0,1:T(8,128)(2,1)S(1)} %concatenate.16, s32[16384]{0:T(1024)S(1)} %fusion.103), kind=kCustom, calls=%fused_computation.1.clone.1 | custom fusion | bytes 8454144 | tf_op jit(solution)/shard_map/while/body/eval_jaxpr/gather | solution.py:53
  122.2 57.4 %gather_fusion.1 = bf16[16384,128]{1,0:T(8,128)(2,1)} fusion(bf16[128,256]{0,1:T(8,128)(2,1)S(1)} %concatenate.16, s32[16384]{0:T(1024)S(1)} %fusion.105), kind=kCustom, calls=%fused_computation.clone.1 | custom fusion | bytes 8454144 | tf_op jit(solution)/shard_map/while/body/eval_jaxpr/gather | solution.py:52
  195.0 57.4 %gather_fusion = bf16[16384,128]{1,0:T(8,128)(2,1)} fusion(bf16[128,256]{0,1:T(8,128)(2,1)S(1)} %concatenate.16, s32[16384]{0:T(1024)S(1)} %fusion.103), kind=kCustom, calls=%fused_computation.1.clone.1 | custom fusion | bytes 8454144 | tf_op jit(solution)/shard_map/while/body/eval_jaxpr/gather | solution.py:53
  263.8 57.4 %gather_fusion.1 = bf16[16384,128]{1,0:T(8,128)(2,1)} fusion(bf16[128,256]{0,1:T(8,128)(2,1)S(1)} %concatenate.16, s32[16384]{0:T(1024)S(1)} %fusion.105), kind=kCustom, calls=%fused_computation.clone.1 | custom fusion | bytes 8454144 | tf_op jit(solution)/shard_map/while/body/eval_jaxpr/gather | solution.py:52
  336.5 57.4 %gather_fusion = bf16[16384,128]{1,0:T(8,128)(2,1)} fusion(bf16[128,256]{0,1:T(8,128)(2,1)S(1)} %concatenate.16, s32[16384]{0:T(1024)S(1)} %fusion.103), kind=kCustom, calls=%fused_computation.1.clone.1 | custom fusion | bytes 8454144 | tf_op jit(solution)/shard_map/while/body/eval_jaxpr/gather | solution.py:53
  405.3 57.4 %gather_fusion.1 = bf16[16384,128]{1,0:T(8,128)(2,1)} fusion(bf16[128,256]{0,1:T(8,128)(2,1)S(1)} %concatenate.16, s32[16384]{0:T(1024)S(1)} %fusion.105), kind=kCustom, calls=%fused_computation.clone.1 | custom fusion | bytes 8454144 | tf_op jit(solution)/shard_map/while/body/eval_jaxpr/gather | solution.py:52
  478.1 57.4 %gather_fusion = bf16[16384,128]{1,0:T(8,128)(2,1)} fusion(bf16[128,256]{0,1:T(8,128)(2,1)S(1)} %concatenate.16, s32[16384]{0:T(1024)S(1)} %fusion.103), kind=kCustom, calls=%fused_computation.1.clone.1 | custom fusion | bytes 8454144 | tf_op jit(solution)/shard_map/while/body/eval_jaxpr/gather | solution.py:53
  546.9 57.4 %gather_fusion.1 = bf16[16384,128]{1,0:T(8,128)(2,1)} fusion(bf16[128,256]{0,1:T(8,128)(2,1)S(1)} %concatenate.16, s32[16384]{0:T(1024)S(1)} %fusion.105), kind=kCustom, calls=%fused_computation.clone.1 | custom fusion | bytes 8454144 | tf_op jit(solution)/shard_map/while/body/eval_jaxpr/gather | solution.py:52
  619.6 57.4 %gather_fusion = bf16[16384,128]{1,0:T(8,128)(2,1)} fusion(bf16[128,256]{0,1:T(8,128)(2,1)S(1)} %concatenate.16, s32[16384]{0:T(1024)S(1)} %fusion.103), kind=kCustom, calls=%fused_computation.1.clone.1 | custom fusion | bytes 8454144 | tf_op jit(solution)/shard_map/while/body/eval_jaxpr/gather | solution.py:53
  688.5 57.4 %gather_fusion.1 = bf16[16384,128]{1,0:T(8,128)(2,1)} fusion(bf16[128,256]{0,1:T(8,128)(2,1)S(1)} %concatenate.16, s32[16384]{0:T(1024)S(1)} %fusion.105), kind=kCustom, calls=%fused_computation.clone.1 | custom fusion | bytes 8454144 | tf_op jit(solution)/shard_map/while/body/eval_jaxpr/gather | solution.py:52
  761.2 57.4 %gather_fusion = bf16[16384,128]{1,0:T(8,128)(2,1)} fusion(bf16[128,256]{0,1:T(8,128)(2,1)S(1)} %concatenate.16, s32[16384]{0:T(1024)S(1)} %fusion.103), kind=kCustom, calls=%fused_computation.1.clone.1 | custom fusion | bytes 8454144 | tf_op jit(solution)/shard_map/while/body/eval_jaxpr/gather | solution.py:53
  830.0 57.4 %gather_fusion.1 = bf16[16384,128]{1,0:T(8,128)(2,1)} fusion(bf16[128,256]{0,1:T(8,128)(2,1)S(1)} %concatenate.16, s32[16384]{0:T(1024)S(1)} %fusion.105), kind=kCustom, calls=%fused_computation.clone.1 | custom fusion | bytes 8454144 | tf_op jit(solution)/shard_map/while/body/eval_jaxpr/gather | solution.py:52
  902.8 57.4 %gather_fusion = bf16[16384,128]{1,0:T(8,128)(2,1)} fusion(bf16[128,256]{0,1:T(8,128)(2,1)S(1)} %concatenate.16, s32[16384]{0:T(1024)S(1)} %fusion.103), kind=kCustom, calls=%fused_computation.1.clone.1 | custom fusion | bytes 8454144 | tf_op jit(solution)/shard_map/while/body/eval_jaxpr/gather | solution.py:53
  971.6 57.4 %gather_fusion.1 = bf16[16384,128]{1,0:T(8,128)(2,1)} fusion(bf16[128,256]{0,1:T(8,128)(2,1)S(1)} %concatenate.16, s32[16384]{0:T(1024)S(1)} %fusion.105), kind=kCustom, calls=%fused_computation.clone.1 | custom fusion | bytes 8454144 | tf_op jit(solution)/shard_map/while/body/eval_jaxpr/gather | solution.py:52
  1044.3 57.4 %gather_fusion = bf16[16384,128]{1,0:T(8,128)(2,1)} fusion(bf16[128,256]{0,1:T(8,128)(2,1)S(1)} %concatenate.16, s32[16384]{0:T(1024)S(1)} %fusion.103), kind=kCustom, calls=%fused_computation.1.clone.1 | custom fusion | bytes 8454144 | tf_op jit(solution)/shard_map/while/body/eval_jaxpr/gather | solution.py:53
  1113.1 57.4 %gather_fusion.1 = bf16[16384,128]{1,0:T(8,128)(2,1)} fusion(bf16[128,256]{0,1:T(8,128)(2,1)S(1)} %concatenate.16, s32[16384]{0:T(1024)S(1)} %fusion.105), kind=kCustom, calls=%fused_computation.clone.1 | custom fusion | bytes 8454144 | tf_op jit(solution)/shard_map/while/body/eval_jaxpr/gather | solution.py:52
  1249.6 253.1 %all-reduce.3.cloned.1.call-done = bf16[1024,4096]{1,0:T(8,128)(2,1)} async-done(((bf16[1024,4096]{1,0:T(8,128)(2,1)}), bf16[1024,4096]{1,0:T(8,128)(2,1)}) %all-reduce.3.cloned.1.call-update) | async-done | bytes 8388624 | tf_op jit(solution)/shard_map/psum | solution.py:160
  1513.9 115.0 %all-gather.10.cloned.1.call-done = bf16[3,4096,1024]{2,1,0:T(8,128)(2,1)} async-done(((bf16[3,512,1024]{2,1,0:T(8,128)(2,1)}), bf16[3,4096,1024]{2,1,0:T(8,128)(2,1)}) %all-gather.10.cloned.1.call-update) | async-done | bytes 25165840 | tf_op jit(solution)/shard_map/all_gather | solution.py:176
  1628.9 32.4 %convert_bitcast_fusion = bf16[3,1024,1024]{2,1,0:T(8,128)(2,1)S(1)} fusion(bf16[3,4096,1024]{2,1,0:T(8,128)(2,1)} %all-gather.10.cloned.1.call-done, bf16[1024,4096]{1,0:T(8,128)(2,1)} %get-tuple-element.355, f32[4096]{0:T(1024)S(1)} %convert_element_type.97, f32[1024]{0:T(1024)S(1)} %add_rsqrt_fusion), kind=kOutput, calls=%fused_computation.78 | convolution fusion | flops 25789726720 | bytes 39866368 | tf_op jit(solution)/shard_map/tr,krc->ktc/dot_general | solution.py:173
  1688.6 657.0 %while.52 = (s32[]{:T(128)}, f32[8,8,128,128]{2,1,3,0:T(8,128)}, s32[8]{0:T(128)S(1)}, f32[8,128,1024]{1,0,2:T(8,128)}, f32[128,1024]{0,1:T(8,128)}, /*index=5*/s32[]{:T(128)}, s32[1]{0:T(128)}, s32[]{:T(128)}, s32[]{:T(128)}) while((s32[]{:T(128)}, f32[8,8,128,128]{2,1,3,0:T(8,128)}, s32[8]{0:T(128)S(1)}, ...), condition=%wide.region_10.11_spmd.clone, body=%wide.region_9.10_spmd.clone.sunk | while | flops 203489280 | bytes 43417768 | solution.py:122
  1690.8 54.4 %gather_fusion.2 = f32[16384,128]{1,0:T(8,128)} fusion(f32[128,128]{1,0:T(8,128)S(1)} %copy.91, s32[16384]{0:T(1024)S(1)} %bitcast_clamp_fusion.2), kind=kCustom, calls=%fused_computation.2.clone.clone.1 | custom fusion | bytes 16842752 | tf_op jit(solution)/shard_map/while/body/eval_jaxpr/gather | solution.py:116
  1772.9 54.4 %gather_fusion.2 = f32[16384,128]{1,0:T(8,128)} fusion(f32[128,128]{1,0:T(8,128)S(1)} %copy.91, s32[16384]{0:T(1024)S(1)} %bitcast_clamp_fusion.2), kind=kCustom, calls=%fused_computation.2.clone.clone.1 | custom fusion | bytes 16842752 | tf_op jit(solution)/shard_map/while/body/eval_jaxpr/gather | solution.py:116
  1855.1 54.4 %gather_fusion.2 = f32[16384,128]{1,0:T(8,128)} fusion(f32[128,128]{1,0:T(8,128)S(1)} %copy.91, s32[16384]{0:T(1024)S(1)} %bitcast_clamp_fusion.2), kind=kCustom, calls=%fused_computation.2.clone.clone.1 | custom fusion | bytes 16842752 | tf_op jit(solution)/shard_map/while/body/eval_jaxpr/gather | solution.py:116
  1937.2 54.4 %gather_fusion.2 = f32[16384,128]{1,0:T(8,128)} fusion(f32[128,128]{1,0:T(8,128)S(1)} %copy.91, s32[16384]{0:T(1024)S(1)} %bitcast_clamp_fusion.2), kind=kCustom, calls=%fused_computation.2.clone.clone.1 | custom fusion | bytes 16842752 | tf_op jit(solution)/shard_map/while/body/eval_jaxpr/gather | solution.py:116
  2000.9 16.2 fusion.110
  2019.3 54.4 %gather_fusion.2 = f32[16384,128]{1,0:T(8,128)} fusion(f32[128,128]{1,0:T(8,128)S(1)} %copy.91, s32[16384]{0:T(1024)S(1)} %bitcast_clamp_fusion.2), kind=kCustom, calls=%fused_computation.2.clone.clone.1 | custom fusion | bytes 16842752 | tf_op jit(solution)/shard_map/while/body/eval_jaxpr/gather | solution.py:116
  2083.0 16.2 fusion.110
  2101.5 54.4 %gather_fusion.2 = f32[16384,128]{1,0:T(8,128)} fusion(f32[128,128]{1,0:T(8,128)S(1)} %copy.91, s32[16384]{0:T(1024)S(1)} %bitcast_clamp_fusion.2), kind=kCustom, calls=%fused_computation.2.clone.clone.1 | custom fusion | bytes 16842752 | tf_op jit(solution)/shard_map/while/body/eval_jaxpr/gather | solution.py:116
  2183.6 54.4 %gather_fusion.2 = f32[16384,128]{1,0:T(8,128)} fusion(f32[128,128]{1,0:T(8,128)S(1)} %copy.91, s32[16384]{0:T(1024)S(1)} %bitcast_clamp_fusion.2), kind=kCustom, calls=%fused_computation.2.clone.clone.1 | custom fusion | bytes 16842752 | tf_op jit(solution)/shard_map/while/body/eval_jaxpr/gather | solution.py:116
  2247.3 16.2 fusion.110
  2265.7 54.4 %gather_fusion.2 = f32[16384,128]{1,0:T(8,128)} fusion(f32[128,128]{1,0:T(8,128)S(1)} %copy.91, s32[16384]{0:T(1024)S(1)} %bitcast_clamp_fusion.2), kind=kCustom, calls=%fused_computation.2.clone.clone.1 | custom fusion | bytes 16842752 | tf_op jit(solution)/shard_map/while/body/eval_jaxpr/gather | solution.py:116
  (280 shorter events, 578.3 us)
Async XLA Ops:
  7.2 1185.9 %all-gather.8.cloned.1.call-start = ((), (), s32[]{:S(2)}) async-start(), calls=%async_computation.1 | async-start | bytes 9437184 | tf_op jit(solution)/shard_map/all_gather | solution.py:157
  7.9 1241.7 %all-gather.6.cloned.1.call-start = ((), (), s32[]{:S(2)}) async-start(), calls=%async_computation | async-start | bytes 10485760 | tf_op jit(solution)/shard_map/all_gather | solution.py:162
  8.8 3.4 collective-permute-start
  11.2 1491.6 %all-reduce.3.cloned.1.call-start = ((), (), s32[]{:S(2)}) async-start(), calls=%async_computation.2 | async-start | bytes 16777216 | tf_op jit(solution)/shard_map/psum | solution.py:160
  27.5 10.6 copy-start.1
  27.6 10.6 collective-permute-start.1
  1208.7 0.7 copy-start.14
  1208.7 13.0 copy-start.12
  1208.7 13.1 copy-start.10
  1208.8 13.3 copy-start.11
  1208.8 420.1 %all-gather.10.cloned.1.call-start = ((), (), s32[]{:S(2)}) async-start(), calls=%async_computation.3 | async-start | bytes 28311552 | tf_op jit(solution)/shard_map/all_gather | solution.py:176
  1222.0 291.8 %copy-start.5 = (f32[16,1024]{0,1:T(8,128)}, f32[16,1024]{0,1:T(8,128)S(1)}, u32[]{:S(2)}) copy-start(f32[16,1024]{0,1:T(8,128)S(1)} %copy.51) | copy-start | bytes 196612
  1222.8 291.1 %copy-start.3 = (f32[16,1024]{1,0:T(8,128)}, f32[16,1024]{1,0:T(8,128)S(1)}, u32[]{:S(2)}) copy-start(f32[16,1024]{1,0:T(8,128)S(1)} %get-tuple-element.360) | copy-start | bytes 196612
  1223.0 290.9 %copy-start.7 = (f32[16,1024]{0,1:T(8,128)}, f32[16,1024]{0,1:T(8,128)S(1)}, u32[]{:S(2)}) copy-start(f32[16,1024]{0,1:T(8,128)S(1)} %copy.48) | copy-start | bytes 196612
  1661.3 5.3 collective-permute-start.2
  1688.6 657.0 %copy-start.8 = (f32[16,1024]{0,1:T(8,128)S(1)}, f32[16,1024]{0,1:T(8,128)}, u32[]{:S(2)}) copy-start(f32[16,1024]{0,1:T(8,128)} %copy-done.7) | copy-start | bytes 196612
  1688.6 657.0 %copy-start.17 = (f32[128]{0:T(128)S(1)}, f32[128]{0:T(128)}, u32[]{:S(2)}) copy-start(f32[128]{0:T(128)} %iota_subtract_fusion.1) | copy-start | bytes 1540
  2345.6 12.0 copy-start
  2345.7 12.0 copy-start.2
  2345.7 12.0 copy-start.9
  2345.7 21.8 copy-start.4
  2345.7 21.8 copy-start.15
  2354.8 15.7 copy-start.6
  2354.8 15.7 copy-start.16
  2384.2 5.4 copy-start.13
Sparse Core Ops, SparseCore 0:
  9.9 58.6 all-gather.7
  70.1 149.6 all-gather.5
  1208.9 293.7 all-reduce.2
  1504.5 124.3 all-gather.9
where the time goes:
time: 2420 us; the launch traced here: 2410 us
  local copies, waits for them, and re-layouts  1620 us (67%)
  waiting for transfers between devices  369 us (15%)
  matrix products  278 us (11%)
  other arithmetic  73.5 us (3%)
  blocking collectives  34 us (1%)
    gather x16, local copies, waits for them, and re-layouts, toeplitz_pair(): earlier = padded[:, row_index - col_index + tap_count]  513 us
    gather x16, local copies, waits for them, and re-layouts, toeplitz_pair(): nearby = padded[:, (row_index - col_index) % (2 * tap_count)]  512 us
    gather x16, local copies, waits for them, and re-layouts, modal_one_group(): kernel_part[jnp.maximum(row_index - col_index, 0)]  509 us
    psum x1, waiting for transfers between devices, on_device(): lax.psum(partial_value.astype(jnp.bfloat16), 'tp').astype(jnp.float32)  253 us
    dot_general x8, matrix products, modal_one_group(): jnp.einsum('ijg,bjg->big', lower_kernel, input_part, precision=lax.Precis...  130 us
    all_gather x1, waiting for transfers between devices, on_device(): lax.all_gather(in_weight, 'ctx', axis=1, tiled=True)  115 us
  transfers between devices with their start and end apart: 7, of which 2 were waited for; matrix products, arithmetic and copies ran while one was open for 51% of the time, Pallas kernels for 0%

commit v1 on v0

v1 whole, which is shorter than its diff:
```python
import functools
import math

import jax
import jax.numpy as jnp
from jax import lax
from jax.experimental import pallas as pl
from jax.experimental.pallas import tpu as pltpu
from jax.sharding import PartitionSpec as P

EPSILON = 1e-05
LANES = 128
BF = jnp.bfloat16
F32 = jnp.float32


def shifted(x, axis, by):
    size = lax.axis_size(axis)
    pairs = [(i, i + by) for i in range(size) if 0 <= i + by < size]
    return lax.ppermute(x, axis, pairs)


def to_rows(x):
    return x.reshape(-1, LANES)


def spread(x_ref, rows, channels, block, first, which):
    groups = channels // LANES
    for m in which:
        for g in range(groups):
            rows[m, pl.ds(first * groups + g, block, groups), :] = x_ref[
                m, :, g * LANES : (g + 1) * LANES
            ].astype(F32)


def collect(out_ref, rows, channels, block):
    groups = channels // LANES
    for g in range(groups):
        out_ref[:, g * LANES : (g + 1) * LANES] = rows[pl.ds(g, block, groups), :].astype(BF)


def slab(ref, token, groups):
    return ref[pl.ds(pl.multiple_of(token * groups, groups), groups), :]


def fir_kernel(
    taps, unit, x_ref, xin_ref, gin_ref, w_ref, f_ref, out_ref, xout_ref, gout_ref, rows, gated, result
):
    block, channels = out_ref.shape
    groups = channels // LANES
    step = pl.program_id(0)

    @pl.when(step == 0)
    def _():
        for m in range(3):
            rows[m, : 2 * groups] = xin_ref[m]
        gated[: taps * groups] = gin_ref[...]

    @pl.when(step > 0)
    def _():
        for m in range(3):
            rows[m, : 2 * groups] = rows[m, block * groups : (block + 2) * groups]
        gated[: taps * groups] = gated[block * groups : (block + taps) * groups]

    spread(x_ref, rows, channels, block, 2, (0, 1, 2))

    def feature(m, token):
        total = None
        for j in range(3):
            start = pl.multiple_of((token + 2 - j) * groups, groups)
            term = w_ref[(3 * m + j) * groups : (3 * m + j + 1) * groups] * rows[m, pl.ds(start, groups), :]
            total = term if total is None else total + term
        return total

    def gate(i, carry):
        for u in range(8):
            token = i * 8 + u
            value = (feature(1, token) * feature(2, token)).astype(BF).astype(F32)
            gated[pl.ds(pl.multiple_of((token + taps) * groups, groups), groups), :] = value
        return carry

    lax.fori_loop(0, block // 8, gate, 0)

    span = 32

    def outputs(i, carry):
        base = i * unit

        def some_taps(part, totals):
            totals = list(totals)
            first = base + taps - part * span
            window = [slab(gated, first + u, groups) for u in range(unit)]
            for j in range(span):
                weight = slab(f_ref, part * span + j, groups)
                for u in range(unit):
                    totals[u] = totals[u] + weight * window[u]
                if j + 1 < span:
                    window = [slab(gated, first - j - 1, groups)] + window[:-1]
            return tuple(totals)

        zero = jnp.zeros((groups, LANES), F32)
        totals = lax.fori_loop(0, taps // span, some_taps, (zero,) * unit)
        for u in range(unit):
            token = base + u
            result[pl.ds(pl.multiple_of(token * groups, groups), groups), :] = (
                feature(0, token) * totals[u]
            )
        return carry

    lax.fori_loop(0, block // unit, outputs, 0)
    collect(out_ref, result, channels, block)

    @pl.when(step == pl.num_programs(0) - 1)
    def _():
        for m in range(3):
            xout_ref[m] = rows[m, block * groups : (block + 2) * groups]
        gout_ref[...] = gated[block * groups : (block + taps) * groups]


def fir(qkv, xin, gin, weights, filters, first, length, block):
    channels = qkv.shape[2]
    groups = channels // LANES
    taps = filters.shape[0] // groups
    offset = first // block
    return pl.pallas_call(
        functools.partial(fir_kernel, taps, 16),
        grid=(length // block,),
        in_specs=[
            pl.BlockSpec((3, block, channels), lambda i: (0, i + offset, 0)),
            pl.BlockSpec(xin.shape, lambda i: (0, 0, 0)),
            pl.BlockSpec(gin.shape, lambda i: (0, 0)),
            pl.BlockSpec(weights.shape, lambda i: (0, 0)),
            pl.BlockSpec(filters.shape, lambda i: (0, 0)),
        ],
        out_specs=[
            pl.BlockSpec((block, channels), lambda i: (i, 0)),
            pl.BlockSpec(xin.shape, lambda i: (0, 0, 0)),
            pl.BlockSpec(gin.shape, lambda i: (0, 0)),
        ],
        out_shape=[
            jax.ShapeDtypeStruct((length, channels), BF),
            jax.ShapeDtypeStruct(xin.shape, F32),
            jax.ShapeDtypeStruct(gin.shape, F32),
        ],
        scratch_shapes=[
            pltpu.VMEM((3, (block + 2) * groups, LANES), F32),
            pltpu.VMEM(((block + taps) * groups, LANES), F32),
            pltpu.VMEM((block * groups, LANES), F32),
        ],
        compiler_params=pltpu.CompilerParams(vmem_limit_bytes=24 * 2**20),
        cost_estimate=pl.CostEstimate(
            flops=2 * taps * length * channels, bytes_accessed=8 * length * channels, transcendentals=0
        ),
        name="medium_filter",
    )(qkv, xin, gin, weights, filters)


def modal_kernel(poles, finish, x_ref, xin_ref, w_ref, p_ref, r_ref, s_ref, d_ref, out_ref, rows, state, result):
    block, channels = x_ref.shape[1:]
    groups = channels // LANES
    step = pl.program_id(0)
    which = (0, 1, 2) if finish else (1, 2)

    @pl.when(step == 0)
    def _():
        for m in which:
            rows[m, : 2 * groups] = xin_ref[m]
        state[...] = s_ref[...]

    @pl.when(step > 0)
    def _():
        for m in which:
            rows[m, : 2 * groups] = rows[m, block * groups : (block + 2) * groups]

    spread(x_ref, rows, channels, block, 2, which)

    def feature(m, token):
        total = None
        for j in range(3):
            start = pl.multiple_of((token + 2 - j) * groups, groups)
            term = w_ref[(3 * m + j) * groups : (3 * m + j + 1) * groups] * rows[m, pl.ds(start, groups), :]
            total = term if total is None else total + term
        return total

    def tokens(i, states):
        states = list(states)
        for u in range(8):
            token = i * 8 + u
            value = (feature(1, token) * feature(2, token)).astype(BF).astype(F32)
            sums = [d_ref[...] * value] if finish else []
            for n in range(poles):
                at = slice(n * groups, (n + 1) * groups)
                states[n] = p_ref[at] * states[n] + value
                if finish:
                    term = r_ref[at] * states[n]
                    if n < 3:
                        sums.append(term)
                    else:
                        sums[n % 4] = sums[n % 4] + term
            if finish:
                result[pl.ds(pl.multiple_of(token * groups, groups), groups), :] = feature(0, token) * (
                    (sums[0] + sums[1]) + (sums[2] + sums[3])
                )
        return tuple(states)

    held = tuple(state[n * groups : (n + 1) * groups] for n in range(poles))
    held = lax.fori_loop(0, block // 8, tokens, held)
    for n in range(poles):
        state[n * groups : (n + 1) * groups] = held[n]
    if finish:
        collect(out_ref, result, channels, block)
    else:

        @pl.when(step == pl.num_programs(0) - 1)
        def _():
            out_ref[...] = state[...]


def modal(qkv, xin, weights, decay, residues, state, skip, block, finish):
    _, length, channels = qkv.shape
    groups = channels // LANES
    poles = decay.shape[0] // groups

    def whole(a):
        return pl.BlockSpec(a.shape, lambda i: (0,) * a.ndim)

    if finish:
        out_spec = pl.BlockSpec((block, channels), lambda i: (i, 0))
        out_shape = jax.ShapeDtypeStruct((length, channels), BF)
    else:
        out_spec = whole(state)
        out_shape = jax.ShapeDtypeStruct(state.shape, F32)
    return pl.pallas_call(
        functools.partial(modal_kernel, poles, finish),
        grid=(length // block,),
        in_specs=[pl.BlockSpec((3, block, channels), lambda i: (0, i, 0))]
        + [whole(a) for a in (xin, weights, decay, residues, state, skip)],
        out_specs=out_spec,
        out_shape=out_shape,
        scratch_shapes=[
            pltpu.VMEM((3, (block + 2) * groups, LANES), F32),
            pltpu.VMEM(state.shape, F32),
            pltpu.VMEM((block * groups, LANES), F32),
        ],
        compiler_params=pltpu.CompilerParams(vmem_limit_bytes=24 * 2**20),
        cost_estimate=pl.CostEstimate(
            flops=4 * poles * length * channels, bytes_accessed=8 * length * channels, transcendentals=0
        ),
        name="modal_finish" if finish else "modal_ends",
    )(qkv, xin, weights, decay, residues, state, skip)


def gate_tail(qkv, weights, count):
    length = qkv.shape[1]
    wide = qkv[1:, length - count - 2 :].astype(F32)
    features = (
        weights[1:, 0][:, None] * wide[:, 2:]
        + weights[1:, 1][:, None] * wide[:, 1:-1]
        + weights[1:, 2][:, None] * wide[:, :-2]
    )
    return (features[0] * features[1]).astype(BF)


def on_device(
    chunk_count,
    qkv_first,
    short_first,
    medium_filter,
    out_weight,
    residual_in,
    norm_gain,
    in_weight,
    short_second,
    rates,
    residues,
    skip_gain,
):
    _, length, channels = qkv_first.shape
    taps = medium_filter.shape[1]
    width = channels * lax.axis_size("tp")
    block = math.gcd(length // chunk_count, 128)

    rim = shifted(qkv_first[:, length - 2 :], "ctx", 1)
    gated_rim = shifted(gate_tail(qkv_first, short_first, taps), "ctx", 1)
    out_all = lax.all_gather(out_weight, "ctx", axis=1, tiled=True)
    in_all = lax.all_gather(in_weight, "ctx", axis=1, tiled=True)
    gain_all = lax.all_gather(norm_gain, "tp", axis=0, tiled=True).astype(F32)

    x_tail = rim.astype(F32).reshape(3, -1, LANES)
    g_tail = to_rows(gated_rim.astype(F32))
    first_taps = to_rows(short_first)
    filter_rows = to_rows(medium_filter.astype(F32).T)

    part = length // chunk_count
    hidden_parts, second_parts = [], []
    for c in range(chunk_count):
        mixed_first, x_tail, g_tail = fir(
            qkv_first, x_tail, g_tail, first_taps, filter_rows, c * part, part, block
        )
        partial_value = jnp.dot(mixed_first, out_all, preferred_element_type=F32).astype(BF)
        summed = lax.psum_scatter(partial_value, "tp", scatter_dimension=1, tiled=True)
        residual = residual_in[c * part : (c + 1) * part]
        hidden = (residual.astype(F32) + summed.astype(F32)).astype(BF)
        hidden_parts.append(hidden)
        hidden_values = lax.all_gather(hidden, "tp", axis=1, tiled=True).astype(F32)
        squares = jnp.sum(hidden_values * hidden_values, axis=1)
        inverse_rms = lax.rsqrt(squares / width + EPSILON)
        normed = (hidden_values * inverse_rms[:, None] * gain_all).astype(BF)
        second_parts.append(
            jnp.einsum("tr,krc->ktc", normed, in_all, preferred_element_type=F32).astype(BF)
        )
    hidden = jnp.concatenate(hidden_parts, axis=0)
    qkv_second = jnp.concatenate(second_parts, axis=1)

    second_rim = shifted(qkv_second[:, length - 2 :], "ctx", 1).astype(F32).reshape(3, -1, LANES)
    second_taps = to_rows(short_second)
    decay = to_rows(jnp.exp(-rates))
    residue_rows = to_rows(residues)
    skip = to_rows(skip_gain)
    step_block = math.gcd(length, 256)
    ends = modal(
        qkv_second, second_rim, second_taps, decay, residue_rows, jnp.zeros_like(decay), skip, step_block, False
    )
    place = lax.axis_index("ctx")
    ends_all = lax.all_gather(ends, "ctx")
    laps = place - 1 - jnp.arange(lax.axis_size("ctx"), dtype=jnp.int32)
    passed = jnp.exp(-to_rows(rates)[None] * (jnp.maximum(laps, 0) * length).astype(F32)[:, None, None])
    state_in = jnp.sum(jnp.where((laps >= 0)[:, None, None], passed * ends_all, 0.0), axis=0)
    mixed = modal(
        qkv_second, second_rim, second_taps, decay, residue_rows, state_in, skip, step_block, True
    )
    return (hidden, mixed)


def solution(mesh):
    placed = (
        P(None, "ctx", "tp"),
        P(None, None, "tp"),
        P("tp", None),
        P("tp", "ctx"),
        P("ctx", "tp"),
        P("tp"),
        P(None, "ctx", "tp"),
        P(None, None, "tp"),
        P(None, "tp"),
        P(None, "tp"),
        P("tp"),
    )
    return jax.shard_map(
        functools.partial(on_device, 4),
        mesh=mesh,
        in_specs=placed,
        out_specs=(P("ctx", "tp"), P("ctx", "tp")),
        check_vma=False,
    )
```

time: 2420 us -> 676 us (0.28)
  local copies, waits for them, and re-layouts: 1620 us -> 8.41 us
  matrix products: 278 us -> 77.1 us
  waiting for transfers between devices: 369 us -> 450 us
  Pallas kernels: 0 us -> 74.7 us
  other arithmetic: 73.5 us -> 18.4 us
    gather x48 -> x0, local copies, waits for them, and re-layouts: 1530 us -> none  [the longest x16 513 us: toeplitz_pair(): earlier = padded[:, row_index - col_index + tap_count]]
    psum x1 -> x0, waiting for transfers between devices: 253 us -> none  [on_device(): lax.psum(partial_value.astype(jnp.bfloat16), 'tp').astype(jnp.float32)]
    dot_general x28 -> x8, matrix products: 278 us -> 77.1 us  [the longest x4 48.3 us: on_device(): jnp.einsum('tr,krc->ktc', normed, in_all, preferred_element_type=F32)]
    all_gather x3 -> x6, waiting for transfers between devices: 115 us -> 285 us  [the longest x4 161 us: on_device(): hidden_values = lax.all_gather(hidden, 'tp', axis=1, tiled=True).astype(F32)]
    reduce_scatter x0 -> x4, waiting for transfers between devices: none -> 161 us  [on_device(): lax.psum_scatter(partial_value, 'tp', scatter_dimension=1, tiled=True)]
    pallas_call x0 -> x6, Pallas kernels: none -> 74.7 us  [the longest x4 46.6 us: fir(): pl.pallas_call(functools.partial(fir_kernel, taps, 16), grid=(length // b...]
    dynamic_slice x73 -> x0, local copies, waits for them, and re-layouts: 38.9 us -> none  [the longest x16 10.2 us: medium_one_group(): lax.dynamic_slice_in_dim(previous_rows, lower, group_size, 2)]
    convert_element_type x10 -> x5, other arithmetic: 33.9 us -> 4.8 us  [the longest x1 3.53 us: on_device(): hidden = (residual.astype(F32) + summed.astype(F32)).astype(BF)]
  transfers between devices with their start and end apart: 7 -> 13, of which waited for: 2 -> 10; matrix products, arithmetic and copies ran while one was open for 51% -> 11% of each run, Pallas kernels for 0% -> 7%
where the time goes in v1:
time: 676 us; the launch traced here: 675 us
  waiting for transfers between devices  450 us (67%)
  matrix products  77.1 us (11%)
  Pallas kernels  74.7 us (11%)
  blocking collectives  21.8 us (3%)
  other arithmetic  18.4 us (3%)
  between operations  14.7 us (2%)
  starting transfers between devices  9.95 us (1%)
  local copies, waits for them, and re-layouts  8.41 us (1%)
    all_gather x4, waiting for transfers between devices, on_device(): hidden_values = lax.all_gather(hidden, 'tp', axis=1, tiled=True).astype(F32)  161 us
    reduce_scatter x4, waiting for transfers between devices, on_device(): lax.psum_scatter(partial_value, 'tp', scatter_dimension=1, tiled=True)  161 us
    all_gather x1, waiting for transfers between devices, on_device(): in_all = lax.all_gather(in_weight, 'ctx', axis=1, tiled=True)  124 us
    dot_general x4, matrix products, on_device(): jnp.einsum('tr,krc->ktc', normed, in_all, preferred_element_type=F32)  48.3 us
    pallas_call x4, Pallas kernels, fir(): pl.pallas_call(functools.partial(fir_kernel, taps, 16), grid=(length // b...  46.6 us
    dot_general x4, matrix products, on_device(): jnp.dot(mixed_first, out_all, preferred_element_type=F32).astype(BF)  28.8 us
    pallas_call x2, Pallas kernels, modal(): pl.pallas_call(functools.partial(modal_kernel, poles, finish), grid=(leng...  28.1 us
  transfers between devices with their start and end apart: 13, of which 10 were waited for; matrix products, arithmetic and copies ran while one was open for 11% of the time, Pallas kernels for 7%

profile of v1, /device:TPU:0, one launch (start us, length us, event | category | flops | bytes accessed | tf_op | source)
XLA Modules:
  0.0 675.4 jit_solution(14298070361972722459)
XLA Ops:
  10.5 2.4 collective-permute-start.1
  13.7 4.5 collective-permute-start
  19.2 3.3 copy-done
  22.5 11.4 %medium_filter.4 = (bf16[256,1024]{1,0:T(8,128)(2,1)S(1)}, f32[3,16,128]{2,1,0:T(8,128)S(1)}, f32[1024,128]{1,0:T(8,128)S(1)}) custom-call(bf16[3,1024,1024]{2,1,0:T(8,128)(2,1)S(1)} %copy-done, f32[3,16,128]{2,1,0:T(8,128)S(1)} %reshape.94.xin_ref, f32[1024,128]{1,0:T(8,128)S(1)} %reshape.96.gin_ref, f32[72,128]{1,0:T(8,128)S(1)} %reshape.84.w_ref, ...), custom_call_target="tpu_custom_call" | custom-call | flops 67108864 | bytes 2097152 | tf_op jit(solution)/shard_map/medium_filter/pallas_call | solution.py:125
  33.9 11.5 %medium_filter.5 = (bf16[256,1024]{1,0:T(8,128)(2,1)S(1)}, f32[3,16,128]{2,1,0:T(8,128)S(1)}, f32[1024,128]{1,0:T(8,128)S(1)}) custom-call(bf16[3,1024,1024]{2,1,0:T(8,128)(2,1)S(1)} %copy-done, f32[3,16,128]{2,1,0:T(8,128)S(1)} %get-tuple-element.13.xin_ref, f32[1024,128]{1,0:T(8,128)S(1)} %get-tuple-element.14.gin_ref, f32[72,128]{1,0:T(8,128)S(1)} %reshape.84.w_ref, ...), custom_call_target="tpu_custom_call" | custom-call | flops 67108864 | bytes 2097152 | tf_op jit(solution)/shard_map/medium_filter/pallas_call | solution.py:125
  45.4 11.5 %medium_filter.6 = (bf16[256,1024]{1,0:T(8,128)(2,1)S(1)}, f32[3,16,128]{2,1,0:T(8,128)S(1)}, f32[1024,128]{1,0:T(8,128)S(1)}) custom-call(bf16[3,1024,1024]{2,1,0:T(8,128)(2,1)S(1)} %copy-done, f32[3,16,128]{2,1,0:T(8,128)S(1)} %get-tuple-element.16.xin_ref, f32[1024,128]{1,0:T(8,128)S(1)} %get-tuple-element.17.gin_ref, f32[72,128]{1,0:T(8,128)S(1)} %reshape.84.w_ref, ...), custom_call_target="tpu_custom_call" | custom-call | flops 67108864 | bytes 2097152 | tf_op jit(solution)/shard_map/medium_filter/pallas_call | solution.py:125
  56.9 12.2 %medium_filter.7 = (bf16[256,1024]{1,0:T(8,128)(2,1)S(1)}, f32[3,16,128]{2,1,0:T(8,128)}, f32[1024,128]{1,0:T(8,128)}) custom-call(bf16[3,1024,1024]{2,1,0:T(8,128)(2,1)S(1)} %copy-done, f32[3,16,128]{2,1,0:T(8,128)S(1)} %get-tuple-element.19.xin_ref, f32[1024,128]{1,0:T(8,128)S(1)} %get-tuple-element.20.gin_ref, f32[72,128]{1,0:T(8,128)S(1)} %reshape.84.w_ref, ...), custom_call_target="tpu_custom_call" | custom-call | flops 67108864 | bytes 2097152 | tf_op jit(solution)/shard_map/medium_filter/pallas_call | solution.py:125
  69.1 7.1 %convolution_convert_fusion = bf16[256,4096]{1,0:T(8,128)(2,1)} fusion(bf16[256,1024]{1,0:T(8,128)(2,1)S(1)} %get-tuple-element.21, bf16[1024,4096]{1,0:T(8,128)(2,1)} %all-gather.8.cloned.1.call-done), kind=kOutput, calls=%fused_computation.9 | convolution fusion | flops 2148532224 | bytes 11010048 | tf_op jit(solution)/shard_map/dot_general | solution.py:300
  76.3 7.1 %convolution_convert_fusion.1 = bf16[256,4096]{1,0:T(8,128)(2,1)} fusion(bf16[256,1024]{1,0:T(8,128)(2,1)S(1)} %get-tuple-element.18, bf16[1024,4096]{1,0:T(8,128)(2,1)} %all-gather.8.cloned.1.call-done), kind=kOutput, calls=%fused_computation.10 | convolution fusion | flops 2148532224 | bytes 11010048 | tf_op jit(solution)/shard_map/dot_general | solution.py:300
  83.4 7.4 %convolution_convert_fusion.2 = bf16[256,4096]{1,0:T(8,128)(2,1)} fusion(bf16[256,1024]{1,0:T(8,128)(2,1)S(1)} %get-tuple-element.15, bf16[1024,4096]{1,0:T(8,128)(2,1)} %all-gather.8.cloned.1.call-done), kind=kOutput, calls=%fused_computation.11 | convolution fusion | flops 2148532224 | bytes 11010048 | tf_op jit(solution)/shard_map/dot_general | solution.py:300
  91.1 7.2 %convolution_convert_fusion.3 = bf16[256,4096]{1,0:T(8,128)(2,1)} fusion(bf16[256,1024]{1,0:T(8,128)(2,1)S(1)} %get-tuple-element.12, bf16[1024,4096]{1,0:T(8,128)(2,1)} %all-gather.8.cloned.1.call-done), kind=kOutput, calls=%fused_computation.12 | convolution fusion | flops 2148532224 | bytes 11010048 | tf_op jit(solution)/shard_map/dot_general | solution.py:300
  98.4 23.7 %reduce-scatter.11.cloned.1.call-done = bf16[256,1024]{1,0:T(8,128)(2,1)} async-done(((bf16[256,4096]{1,0:T(8,128)(2,1)}), bf16[256,1024]{1,0:T(8,128)(2,1)}) %reduce-scatter.11.cloned.1.call-update) | async-done | bytes 524304 | tf_op jit(solution)/shard_map/reduce_scatter | solution.py:301
  122.1 45.6 %reduce-scatter.9.cloned.1.call-done = bf16[256,1024]{1,0:T(8,128)(2,1)} async-done(((bf16[256,4096]{1,0:T(8,128)(2,1)}), bf16[256,1024]{1,0:T(8,128)(2,1)}) %reduce-scatter.9.cloned.1.call-update) | async-done | bytes 524304 | tf_op jit(solution)/shard_map/reduce_scatter | solution.py:301
  167.7 45.9 %reduce-scatter.7.cloned.1.call-done = bf16[256,1024]{1,0:T(8,128)(2,1)} async-done(((bf16[256,4096]{1,0:T(8,128)(2,1)}), bf16[256,1024]{1,0:T(8,128)(2,1)}) %reduce-scatter.7.cloned.1.call-update) | async-done | bytes 524304 | tf_op jit(solution)/shard_map/reduce_scatter | solution.py:301
  213.7 46.0 %reduce-scatter.5.cloned.1.call-done = bf16[256,1024]{1,0:T(8,128)(2,1)} async-done(((bf16[256,4096]{1,0:T(8,128)(2,1)}), bf16[256,1024]{1,0:T(8,128)(2,1)}) %reduce-scatter.5.cloned.1.call-update) | async-done | bytes 524304 | tf_op jit(solution)/shard_map/reduce_scatter | solution.py:301
  259.7 3.5 add_convert_fusion.3
  266.1 12.0 %all_gather.29 = bf16[4096]{0:T(1024)(128)(2,1)S(1)} all-gather(bf16[1024]{0:T(1024)(128)(2,1)S(1)} %copy-done.16), channel_id=1, replica_groups=mesh['ctx'=8,'tp'=4] {'tp'}, dimensions={0}, use_global_device_ids=true | all-gather | bytes 10240 | tf_op jit(solution)/shard_map/all_gather | solution.py:287
  279.9 29.1 %all-gather.10.cloned.1.call-done = bf16[256,4096]{1,0:T(8,128)(2,1)} async-done(((bf16[256,1024]{1,0:T(8,128)(2,1)}), bf16[256,4096]{1,0:T(8,128)(2,1)}) %all-gather.10.cloned.1.call-update) | async-done | bytes 2097168 | tf_op jit(solution)/shard_map/all_gather | solution.py:305
  311.1 43.9 %all-gather.14.cloned.1.call-done = bf16[256,4096]{1,0:T(8,128)(2,1)} async-done(((bf16[256,1024]{1,0:T(8,128)(2,1)}), bf16[256,4096]{1,0:T(8,128)(2,1)}) %all-gather.14.cloned.1.call-update) | async-done | bytes 2097168 | tf_op jit(solution)/shard_map/all_gather | solution.py:305
  357.1 44.2 %all-gather.16.cloned.1.call-done = bf16[256,4096]{1,0:T(8,128)(2,1)} async-done(((bf16[256,1024]{1,0:T(8,128)(2,1)}), bf16[256,4096]{1,0:T(8,128)(2,1)}) %all-gather.16.cloned.1.call-update) | async-done | bytes 2097168 | tf_op jit(solution)/shard_map/all_gather | solution.py:305
  403.4 44.2 %all-gather.18.cloned.1.call-done = bf16[256,4096]{1,0:T(8,128)(2,1)} async-done(((bf16[256,1024]{1,0:T(8,128)(2,1)}), bf16[256,4096]{1,0:T(8,128)(2,1)}) %all-gather.18.cloned.1.call-update) | async-done | bytes 2097168 | tf_op jit(solution)/shard_map/all_gather | solution.py:305
  449.6 123.7 %all-gather.12.cloned.1.call-done = bf16[3,4096,1024]{2,1,0:T(8,128)(2,1)} async-done(((bf16[3,512,1024]{2,1,0:T(8,128)(2,1)}), bf16[3,4096,1024]{2,1,0:T(8,128)(2,1)}) %all-gather.12.cloned.1.call-update) | async-done | bytes 25165840 | tf_op jit(solution)/shard_map/all_gather | solution.py:286
  573.4 12.2 %fusion.44 = bf16[3,256,1024]{2,1,0:T(8,128)(2,1)S(1)} fusion(bf16[3,4096,1024]{2,1,0:T(8,128)(2,1)} %all-gather.12.cloned.1.call-done, bf16[256,4096]{1,0:T(8,128)(2,1)} %all-gather.18.cloned.1.call-done, f32[256]{0:T(256)S(1)} %add_rsqrt_fusion, f32[4096]{0:T(1024)S(1)} %convert_element_type.139), kind=kOutput, calls=%fused_computation.46 | convolution fusion | flops 6447431680 | bytes 28853248 | tf_op jit(solution)/shard_map/tr,krc->ktc/dot_general | solution.py:310
  585.7 2.5 collective-permute-start.2
  588.2 12.0 %fusion.53 = bf16[3,256,1024]{2,1,0:T(8,128)(2,1)S(1)} fusion(bf16[3,4096,1024]{2,1,0:T(8,128)(2,1)} %all-gather.12.cloned.1.call-done, bf16[256,4096]{1,0:T(8,128)(2,1)S(1)} %copy-done.8, f32[4096]{0:T(1024)S(1)} %convert_element_type.139, f32[256]{0:T(256)S(1)} %add_rsqrt_fusion.3), kind=kOutput, calls=%fused_computation.49 | convolution fusion | flops 6447431680 | bytes 28853248 | tf_op jit(solution)/shard_map/tr,krc->ktc/dot_general | solution.py:310
  600.2 12.1 %fusion.50 = bf16[3,256,1024]{2,1,0:T(8,128)(2,1)S(1)} fusion(bf16[3,4096,1024]{2,1,0:T(8,128)(2,1)} %all-gather.12.cloned.1.call-done, bf16[256,4096]{1,0:T(8,128)(2,1)S(1)} %copy-done.9, f32[256]{0:T(256)S(1)} %add_rsqrt_fusion.2, f32[4096]{0:T(1024)S(1)} %convert_element_type.139), kind=kOutput, calls=%fused_computation.48 | convolution fusion | flops 6447431680 | bytes 28853248 | tf_op jit(solution)/shard_map/tr,krc->ktc/dot_general | solution.py:310
  612.3 12.0 %fusion.47 = bf16[3,256,1024]{2,1,0:T(8,128)(2,1)S(1)} fusion(bf16[3,4096,1024]{2,1,0:T(8,128)(2,1)} %all-gather.12.cloned.1.call-done, bf16[256,4096]{1,0:T(8,128)(2,1)S(1)} %copy-done.10, f32[256]{0:T(256)S(1)} %add_rsqrt_fusion.1, f32[4096]{0:T(1024)S(1)} %convert_element_type.139), kind=kOutput, calls=%fused_computation.47 | convolution fusion | flops 6447431680 | bytes 28853248 | tf_op jit(solution)/shard_map/tr,krc->ktc/dot_general | solution.py:310
  624.3 3.2 pad_maximum_fusion.x_ref
  627.6 2.8 copy-done.1
  630.4 9.6 %modal_ends.1 = f32[128,128]{1,0:T(8,128)S(1)} custom-call(bf16[3,1024,1024]{2,1,0:T(8,128)(2,1)S(1)} %copy-done.1, f32[3,16,128]{2,1,0:T(8,128)S(1)} %reshape.100.xin_ref, f32[72,128]{1,0:T(8,128)S(1)} %reshape.89.w_ref, f32[128,128]{1,0:T(8,128)S(1)} %reshape.90.p_ref, f32[128,128]{1,0:T(8,128)S(1)} %reshape.91.r_ref, ...), custom_call_target="tpu_custom_call" | custom-call | flops 67108864 | bytes 8388608 | tf_op jit(solution)/shard_map/modal_ends/pallas_call | solution.py:233
  639.9 9.8 %all-gather = f32[1024,128]{1,0:T(8,128)S(1)} all-gather(f32[128,128]{1,0:T(8,128)S(1)} %modal_ends.1), channel_id=2, replica_groups=mesh['ctx'=8,'tp'=4] {'ctx'}, dimensions={0}, use_global_device_ids=true | all-gather | bytes 589824 | tf_op jit(solution)/shard_map/all_gather | solution.py:325
  650.0 18.6 %modal_finish.1 = bf16[1024,1024]{1,0:T(8,128)(2,1)} custom-call(bf16[3,1024,1024]{2,1,0:T(8,128)(2,1)S(1)} %copy-done.1, f32[3,16,128]{2,1,0:T(8,128)S(1)} %reshape.100.xin_ref, f32[72,128]{1,0:T(8,128)S(1)} %reshape.89.w_ref, f32[128,128]{1,0:T(8,128)S(1)} %reshape.90.p_ref, f32[128,128]{1,0:T(8,128)S(1)} %reshape.91.r_ref, ...), custom_call_target="tpu_custom_call" | custom-call | flops 67108864 | bytes 8388608 | tf_op jit(solution)/shard_map/modal_finish/pallas_call | solution.py:233
  (90 shorter events, 18.4 us)
Async XLA Ops:
  7.2 11.0 %copy-start.11 = (bf16[1024,128]{1,0:T(8,128)(2,1)S(1)}, bf16[1024,128]{1,0:T(8,128)(2,1)}, u32[]{:S(2)}) copy-start(bf16[1024,128]{1,0:T(8,128)(2,1)} %param.13) | copy-start | bytes 786436
  7.2 61.9 %all-gather.8.cloned.1.call-start = ((), (), s32[]{:S(2)}) async-start(), calls=%async_computation.4 | async-start | bytes 9437184 | tf_op jit(solution)/shard_map/all_gather | solution.py:285
  7.9 10.4 %copy-start.12 = (f32[3,3,1024]{2,1,0:T(4,128)S(1)}, f32[3,3,1024]{2,1,0:T(4,128)}, u32[]{:S(2)}) copy-start(f32[3,3,1024]{2,1,0:T(4,128)} %param.12) | copy-start | bytes 110596
  7.9 114.2 %reduce-scatter.11.cloned.1.call-start = ((), (), s32[]{:S(2)}) async-start(), calls=%async_computation.8 | async-start | bytes 2621440 | tf_op jit(solution)/shard_map/reduce_scatter | solution.py:301
  10.5 8.5 %collective-permute-start.1 = (bf16[128,1024]{1,0:T(8,128)(2,1)S(1)}, bf16[128,1024]{1,0:T(8,128)(2,1)S(1)}, u32[]{:S(2)}, u32[]{:S(2)}) collective-permute-start(bf16[128,1024]{1,0:T(8,128)(2,1)S(1)} %fusion.59), channel_id=1, source_target_pairs={{0,4},{4,8},{8,12},{12,16},{16,20},{20,24},{24,28},{1,5},{5,9},{9,... | collective-permute-start | bytes 786440 | tf_op jit(solution)/shard_map/ppermute | solution.py:20
  13.7 5.3 collective-permute-start
  19.2 3.3 copy-start
  76.2 91.5 %reduce-scatter.9.cloned.1.call-start = ((), (), s32[]{:S(2)}) async-start(), calls=%async_computation.7 | async-start | bytes 2621440 | tf_op jit(solution)/shard_map/reduce_scatter | solution.py:301
  83.4 130.3 %reduce-scatter.7.cloned.1.call-start = ((), (), s32[]{:S(2)}) async-start(), calls=%async_computation.6 | async-start | bytes 2621440 | tf_op jit(solution)/shard_map/reduce_scatter | solution.py:301
  90.8 168.9 %reduce-scatter.5.cloned.1.call-start = ((), (), s32[]{:S(2)}) async-start(), calls=%async_computation.5 | async-start | bytes 2621440 | tf_op jit(solution)/shard_map/reduce_scatter | solution.py:301
  91.0 168.6 %copy-start.7 = (bf16[1024,1024]{1,0:T(8,128)(2,1)S(1)}, bf16[1024,1024]{1,0:T(8,128)(2,1)}, u32[]{:S(2)}) copy-start(bf16[1024,1024]{1,0:T(8,128)(2,1)} %param.15) | copy-start | bytes 6291460
  98.3 210.7 %all-gather.10.cloned.1.call-start = ((), (), s32[]{:S(2)}) async-start(), calls=%async_computation.9 | async-start | bytes 2621440 | tf_op jit(solution)/shard_map/all_gather | solution.py:305
  263.2 2.9 copy-start.16
  263.2 14.9 %copy-start.13 = (f32[16,1024]{1,0:T(8,128)S(1)}, f32[16,1024]{1,0:T(8,128)}, u32[]{:S(2)}) copy-start(f32[16,1024]{1,0:T(8,128)} %param.19) | copy-start | bytes 196612
  263.2 15.0 %copy-start.14 = (f32[16,1024]{1,0:T(8,128)S(1)}, f32[16,1024]{1,0:T(8,128)}, u32[]{:S(2)}) copy-start(f32[16,1024]{1,0:T(8,128)} %param.20) | copy-start | bytes 196612
  263.2 15.0 %copy-start.15 = (f32[3,3,1024]{2,1,0:T(4,128)S(1)}, f32[3,3,1024]{2,1,0:T(4,128)}, u32[]{:S(2)}) copy-start(f32[3,3,1024]{2,1,0:T(4,128)} %param.18) | copy-start | bytes 110596
  263.2 15.1 %copy-start.3 = (bf16[256,1024]{1,0:T(8,128)(2,1)S(1)}, bf16[256,1024]{1,0:T(8,128)(2,1)}, u32[]{:S(2)}) copy-start(bf16[256,1024]{1,0:T(8,128)(2,1)} %get-tuple-element.24) | copy-start | bytes 1572868
  263.3 15.1 %copy-start.4 = (bf16[256,1024]{1,0:T(8,128)(2,1)S(1)}, bf16[256,1024]{1,0:T(8,128)(2,1)}, u32[]{:S(2)}) copy-start(bf16[256,1024]{1,0:T(8,128)(2,1)} %get-tuple-element.25) | copy-start | bytes 1572868
  263.3 15.1 %copy-start.5 = (bf16[256,1024]{1,0:T(8,128)(2,1)S(1)}, bf16[256,1024]{1,0:T(8,128)(2,1)}, u32[]{:S(2)}) copy-start(bf16[256,1024]{1,0:T(8,128)(2,1)} %get-tuple-element.23) | copy-start | bytes 1572868
  263.3 15.1 %copy-start.6 = (bf16[256,1024]{1,0:T(8,128)(2,1)S(1)}, bf16[256,1024]{1,0:T(8,128)(2,1)}, u32[]{:S(2)}) copy-start(bf16[256,1024]{1,0:T(8,128)(2,1)} %get-tuple-element.22) | copy-start | bytes 1572868
  263.3 91.7 %all-gather.14.cloned.1.call-start = ((), (), s32[]{:S(2)}) async-start(), calls=%async_computation.11 | async-start | bytes 2621440 | tf_op jit(solution)/shard_map/all_gather | solution.py:305
  264.1 137.2 %all-gather.16.cloned.1.call-start = ((), (), s32[]{:S(2)}) async-start(), calls=%async_computation.12 | async-start | bytes 2621440 | tf_op jit(solution)/shard_map/all_gather | solution.py:305
  264.8 182.7 %all-gather.18.cloned.1.call-start = ((), (), s32[]{:S(2)}) async-start(), calls=%async_computation.13 | async-start | bytes 2621440 | tf_op jit(solution)/shard_map/all_gather | solution.py:305
  265.5 307.8 %all-gather.12.cloned.1.call-start = ((), (), s32[]{:S(2)}) async-start(), calls=%async_computation.10 | async-start | bytes 28311552 | tf_op jit(solution)/shard_map/all_gather | solution.py:286
  449.6 138.5 %copy-start.8 = (bf16[256,4096]{1,0:T(8,128)(2,1)S(1)}, bf16[256,4096]{1,0:T(8,128)(2,1)}, u32[]{:S(2)}) copy-start(bf16[256,4096]{1,0:T(8,128)(2,1)} %all-gather.10.cloned.1.call-done) | copy-start | bytes 6291460
  585.6 14.5 %copy-start.9 = (bf16[256,4096]{1,0:T(8,128)(2,1)S(1)}, bf16[256,4096]{1,0:T(8,128)(2,1)}, u32[]{:S(2)}) copy-start(bf16[256,4096]{1,0:T(8,128)(2,1)} %all-gather.14.cloned.1.call-done) | copy-start | bytes 6291460
  585.7 41.9 %collective-permute-start.2 = (bf16[3,2,1024]{2,1,0:T(2,128)(2,1)S(1)}, bf16[3,2,1024]{2,1,0:T(2,128)(2,1)S(1)}, u32[]{:S(2)}, u32[]{:S(2)}) collective-permute-start(bf16[3,2,1024]{2,1,0:T(2,128)(2,1)S(1)} %slice.65), channel_id=1, source_target_pairs={{0,4},{4,8},{8,12},{12,16},{16,20},{20,24},{24,28},{1,5},{5,9},{9,... | collective-permute-start | bytes 36872 | tf_op jit(solution)/shard_map/ppermute | solution.py:20
  600.2 12.1 %copy-start.10 = (bf16[256,4096]{1,0:T(8,128)(2,1)S(1)}, bf16[256,4096]{1,0:T(8,128)(2,1)}, u32[]{:S(2)}) copy-start(bf16[256,4096]{1,0:T(8,128)(2,1)} %all-gather.16.cloned.1.call-done) | copy-start | bytes 6291460
  624.3 3.2 copy-start.2
  627.6 2.8 copy-start.1
Sparse Core Ops, SparseCore 0:
  9.9 58.6 all-gather.7
  76.4 45.6 reduce-scatter.10
  124.5 43.1 reduce-scatter.8
  170.5 43.1 reduce-scatter.6
  216.5 43.1 reduce-scatter.4
  263.4 45.5 all-gather.9
  310.6 44.4 all-gather.13
  356.6 44.6 all-gather.15
  402.9 44.6 all-gather.17
  449.3 124.0 all-gather.11

commit v2 on v1

--- a/solution.py
+++ b/solution.py
@@ -18,6 +18,22 @@
     size = lax.axis_size(axis)
     pairs = [(i, i + by) for i in range(size) if 0 <= i + by < size]
     return lax.ppermute(x, axis, pairs)
+
+
+def gather_rows(x, axis, ahead):
+    size = lax.axis_size(axis)
+    count = size.bit_length() - 1
+    if size != 1 << count:
+        return lax.all_gather(x, axis, axis=1, tiled=True)
+    place = lax.axis_index(axis)
+    order = [b for b in ahead if b < count] + [b for b in range(count - 1, -1, -1) if b not in ahead]
+    held = x.reshape(x.shape[:1] + (1,) * count + x.shape[1:])
+    for b in order:
+        other = lax.ppermute(held, axis, [(i, i ^ (1 << b)) for i in range(size)])
+        upper = (place >> b) & 1 == 1
+        low, high = jnp.where(upper, other, held), jnp.where(upper, held, other)
+        held = jnp.concatenate([low, high], axis=count - b)
+    return held.reshape(x.shape[0], -1, x.shape[2])
 
 
 def to_rows(x):
@@ -283,7 +299,12 @@
     rim = shifted(qkv_first[:, length - 2 :], "ctx", 1)
     gated_rim = shifted(gate_tail(qkv_first, short_first, taps), "ctx", 1)
     out_all = lax.all_gather(out_weight, "ctx", axis=1, tiled=True)
-    in_all = lax.all_gather(in_weight, "ctx", axis=1, tiled=True)
+    in_weight, out_all = lax.optimization_barrier((in_weight, out_all))
+    half = channels // 2
+    in_halves = (
+        gather_rows(in_weight[:, :, :half], "ctx", (1, 2)),
+        gather_rows(in_weight[:, :, half:], "ctx", (2, 1)),
+    )
     gain_all = lax.all_gather(norm_gain, "tp", axis=0, tiled=True).astype(F32)
 
     x_tail = rim.astype(F32).reshape(3, -1, LANES)
@@ -306,9 +327,10 @@
         squares = jnp.sum(hidden_values * hidden_values, axis=1)
         inverse_rms = lax.rsqrt(squares / width + EPSILON)
         normed = (hidden_values * inverse_rms[:, None] * gain_all).astype(BF)
-        second_parts.append(
-            jnp.einsum("tr,krc->ktc", normed, in_all, preferred_element_type=F32).astype(BF)
-        )
+        products = [
+            jnp.einsum("tr,krc->ktc", normed, w, preferred_element_type=F32).astype(BF) for w in in_halves
+        ]
+        second_parts.append(jnp.concatenate(products, axis=2))
     hidden = jnp.concatenate(hidden_parts, axis=0)
     qkv_second = jnp.concatenate(second_parts, axis=1)
 

time: 676 us -> 686 us (1.015); the launches traced: 675 us -> 676 us
  waiting for transfers between devices: 450 us -> 284 us
  local copies, waits for them, and re-layouts: 8.41 us -> 126 us
  other arithmetic: 18.4 us -> 69.9 us
  matrix products: 77.1 us -> 66.7 us
    all_gather x4, waiting for transfers between devices: 161 us -> 32.2 us  [on_device(): hidden_values = lax.all_gather(hidden, 'tp', axis=1, tiled=True).astype(F32)]
    all_gather x1 -> x0, waiting for transfers between devices: 124 us -> none  [on_device(): in_all = lax.all_gather(in_weight, 'ctx', axis=1, tiled=True)]
    ppermute x0 -> x6, waiting for transfers between devices: none -> 97.7 us  [gather_rows(): other = lax.ppermute(held, axis, [(i, i ^ 1 << b) for i in range(size)])]
    concatenate x0 -> x2, local copies, waits for them, and re-layouts: none -> 63 us  [gather_rows(): held = jnp.concatenate([low, high], axis=count - b)]
    reshape x0 -> x3, local copies, waits for them, and re-layouts: none -> 44.3 us  [the longest x2 42.3 us: gather_rows(): return held.reshape(x.shape[0], -1, x.shape[2])]
    reduce_scatter x4, waiting for transfers between devices: 161 us -> 118 us  [on_device(): lax.psum_scatter(partial_value, 'tp', scatter_dimension=1, tiled=True)]
    all_gather x1, waiting for transfers between devices: 0.01 us -> 34.7 us  [on_device(): out_all = lax.all_gather(out_weight, 'ctx', axis=1, tiled=True)]
    concatenate x0 -> x7, other arithmetic: none -> 27.5 us  [the longest x6 27.5 us: gather_rows(): held = jnp.concatenate([low, high], axis=count - b)]
  transfers between devices with their start and end apart: 13 -> 18, of which waited for: 10 -> 9; matrix products, arithmetic and copies ran while one was open for 11% -> 13% of each run, Pallas kernels for 7% -> 7%
where the time goes in v2:
time: 686 us; the launch traced here: 676 us
  waiting for transfers between devices  284 us (41%)
  local copies, waits for them, and re-layouts  126 us (18%)
  Pallas kernels  74.9 us (11%)
  other arithmetic  69.9 us (10%)
  matrix products  66.7 us (10%)
  blocking collectives  22.9 us (3%)
  starting transfers between devices  15.9 us (2%)
  between operations  14.7 us (2%)
    reduce_scatter x4, waiting for transfers between devices, on_device(): lax.psum_scatter(partial_value, 'tp', scatter_dimension=1, tiled=True)  118 us
    ppermute x6, waiting for transfers between devices, gather_rows(): other = lax.ppermute(held, axis, [(i, i ^ 1 << b) for i in range(size)])  97.7 us
    concatenate x2, local copies, waits for them, and re-layouts, gather_rows(): held = jnp.concatenate([low, high], axis=count - b)  63 us
    pallas_call x4, Pallas kernels, fir(): pl.pallas_call(functools.partial(fir_kernel, taps, 16), grid=(length // b...  46.6 us
    reshape x2, local copies, waits for them, and re-layouts, gather_rows(): return held.reshape(x.shape[0], -1, x.shape[2])  42.3 us
    dot_general x8, matrix products, on_device(): jnp.einsum('tr,krc->ktc', normed, w, preferred_element_type=F32).astype(BF)  38.4 us
    all_gather x1, waiting for transfers between devices, on_device(): out_all = lax.all_gather(out_weight, 'ctx', axis=1, tiled=True)  34.7 us
    all_gather x4, waiting for transfers between devices, on_device(): hidden_values = lax.all_gather(hidden, 'tp', axis=1, tiled=True).astype(F32)  32.2 us
  transfers between devices with their start and end apart: 18, of which 9 were waited for; matrix products, arithmetic and copies ran while one was open for 13% of the time, Pallas kernels for 7%

profile of v2, /device:TPU:0, one launch (start us, length us, event | category | flops | bytes accessed | tf_op | source)
XLA Modules:
  0.0 675.6 jit_solution(9972446973395988654)
XLA Ops:
  13.7 4.5 collective-permute-start
  22.5 11.4 %medium_filter.4 = (bf16[256,1024]{1,0:T(8,128)(2,1)S(1)}, f32[3,16,128]{2,1,0:T(8,128)S(1)}, f32[1024,128]{1,0:T(8,128)S(1)}) custom-call(bf16[3,1024,1024]{2,1,0:T(8,128)(2,1)S(1)} %copy-done, f32[3,16,128]{2,1,0:T(8,128)S(1)} %reshape.110.xin_ref, f32[1024,128]{1,0:T(8,128)S(1)} %reshape.112.gin_ref, f32[72,128]{1,0:T(8,128)S(1)} %reshape.96.w_ref, ...), custom_call_target="tpu_custom_call" | custom-call | flops 67108864 | bytes 2097152 | tf_op jit(solution)/shard_map/medium_filter/pallas_call | solution.py:141
  33.9 34.7 %all-gather.7.cloned.1.call-done = bf16[1024,4096]{1,0:T(8,128)(2,1)} async-done(((bf16[1024,512]{1,0:T(8,128)(2,1)}), bf16[1024,4096]{1,0:T(8,128)(2,1)}) %all-gather.7.cloned.1.call-update) | async-done | bytes 8388624 | tf_op jit(solution)/shard_map/all_gather | solution.py:301
  68.6 7.1 %convolution_convert_fusion.3 = bf16[256,4096]{1,0:T(8,128)(2,1)} fusion(bf16[256,1024]{1,0:T(8,128)(2,1)S(1)} %get-tuple-element.14, bf16[1024,4096]{1,0:T(8,128)(2,1)} %all-gather.7.cloned.1.call-done), kind=kOutput, calls=%fused_computation.20 | convolution fusion | flops 2148532224 | bytes 11010048 | tf_op jit(solution)/shard_map/dot_general | solution.py:321
  78.5 11.4 %medium_filter.5 = (bf16[256,1024]{1,0:T(8,128)(2,1)S(1)}, f32[3,16,128]{2,1,0:T(8,128)S(1)}, f32[1024,128]{1,0:T(8,128)S(1)}) custom-call(bf16[3,1024,1024]{2,1,0:T(8,128)(2,1)S(1)} %copy-done.1, f32[3,16,128]{2,1,0:T(8,128)S(1)} %get-tuple-element.16.xin_ref, f32[1024,128]{1,0:T(8,128)S(1)} %get-tuple-element.17.gin_ref, f32[72,128]{1,0:T(8,128)S(1)} %reshape.96.w_ref, ...), custom_call_target="tpu_custom_call" | custom-call | flops 67108864 | bytes 2097152 | tf_op jit(solution)/shard_map/medium_filter/pallas_call | solution.py:141
  89.9 7.1 %convolution_convert_fusion.2 = bf16[256,4096]{1,0:T(8,128)(2,1)} fusion(bf16[256,1024]{1,0:T(8,128)(2,1)S(1)} %get-tuple-element.18, bf16[1024,4096]{1,0:T(8,128)(2,1)} %all-gather.7.cloned.1.call-done), kind=kOutput, calls=%fused_computation.19 | convolution fusion | flops 2148532224 | bytes 11010048 | tf_op jit(solution)/shard_map/dot_general | solution.py:321
  99.9 11.4 %medium_filter.6 = (bf16[256,1024]{1,0:T(8,128)(2,1)S(1)}, f32[3,16,128]{2,1,0:T(8,128)S(1)}, f32[1024,128]{1,0:T(8,128)S(1)}) custom-call(bf16[3,1024,1024]{2,1,0:T(8,128)(2,1)S(1)} %copy-done.2, f32[3,16,128]{2,1,0:T(8,128)S(1)} %get-tuple-element.19.xin_ref, f32[1024,128]{1,0:T(8,128)S(1)} %get-tuple-element.20.gin_ref, f32[72,128]{1,0:T(8,128)S(1)} %reshape.96.w_ref, ...), custom_call_target="tpu_custom_call" | custom-call | flops 67108864 | bytes 2097152 | tf_op jit(solution)/shard_map/medium_filter/pallas_call | solution.py:141
  111.4 12.3 %medium_filter.7 = (bf16[256,1024]{1,0:T(8,128)(2,1)S(1)}, f32[3,16,128]{2,1,0:T(8,128)}, f32[1024,128]{1,0:T(8,128)}) custom-call(bf16[3,1024,1024]{2,1,0:T(8,128)(2,1)S(1)} %copy-done.2, f32[3,16,128]{2,1,0:T(8,128)S(1)} %get-tuple-element.22.xin_ref, f32[1024,128]{1,0:T(8,128)S(1)} %get-tuple-element.23.gin_ref, f32[72,128]{1,0:T(8,128)S(1)} %reshape.96.w_ref, ...), custom_call_target="tpu_custom_call" | custom-call | flops 67108864 | bytes 2097152 | tf_op jit(solution)/shard_map/medium_filter/pallas_call | solution.py:141
  123.6 7.0 %convolution_convert_fusion = bf16[256,4096]{1,0:T(8,128)(2,1)} fusion(bf16[256,1024]{1,0:T(8,128)(2,1)S(1)} %get-tuple-element.24, bf16[1024,4096]{1,0:T(8,128)(2,1)} %all-gather.7.cloned.1.call-done), kind=kOutput, calls=%fused_computation.17 | convolution fusion | flops 2148532224 | bytes 11010048 | tf_op jit(solution)/shard_map/dot_general | solution.py:321
  131.0 7.2 %convolution_convert_fusion.1 = bf16[256,4096]{1,0:T(8,128)(2,1)} fusion(bf16[256,1024]{1,0:T(8,128)(2,1)S(1)} %get-tuple-element.21, bf16[1024,4096]{1,0:T(8,128)(2,1)} %all-gather.7.cloned.1.call-done), kind=kOutput, calls=%fused_computation.18 | convolution fusion | flops 2148532224 | bytes 11010048 | tf_op jit(solution)/shard_map/dot_general | solution.py:321
  138.3 27.6 %reduce-scatter.7.cloned.1.call-done = bf16[256,1024]{1,0:T(8,128)(2,1)} async-done(((bf16[256,4096]{1,0:T(8,128)(2,1)}), bf16[256,1024]{1,0:T(8,128)(2,1)}) %reduce-scatter.7.cloned.1.call-update) | async-done | bytes 524304 | tf_op jit(solution)/shard_map/reduce_scatter | solution.py:322
  165.9 45.4 %reduce-scatter.11.cloned.1.call-done = bf16[256,1024]{1,0:T(8,128)(2,1)} async-done(((bf16[256,4096]{1,0:T(8,128)(2,1)}), bf16[256,1024]{1,0:T(8,128)(2,1)}) %reduce-scatter.11.cloned.1.call-update) | async-done | bytes 524304 | tf_op jit(solution)/shard_map/reduce_scatter | solution.py:322
  211.3 45.5 %reduce-scatter.9.cloned.1.call-done = bf16[256,1024]{1,0:T(8,128)(2,1)} async-done(((bf16[256,4096]{1,0:T(8,128)(2,1)}), bf16[256,1024]{1,0:T(8,128)(2,1)}) %reduce-scatter.9.cloned.1.call-update) | async-done | bytes 524304 | tf_op jit(solution)/shard_map/reduce_scatter | solution.py:322
  265.9 33.2 %collective-permute-done.2 = bf16[3,1,1,1,512,512]{5,4,0,3,2,1:T(8,128)(2,1)S(1)} collective-permute-done((bf16[3,1,1,1,512,512]{5,4,0,3,2,1:T(8,128)(2,1)}, bf16[3,1,1,1,512,512]{5,4,0,3,2,1:T(8,128)(2,1)S(1)}, u32[]{:S(2)}, u32[]{:S(2)}) %collective-permute-start.2) | collective-permute-done | bytes 1572896 | tf_op jit(solution)/shard_map/ppermute | solution.py:32
  312.3 64.2 %collective-permute-done.6 = bf16[3,2,1,1,512,512]{5,4,0,3,2,1:T(8,128)(2,1)} collective-permute-done((bf16[3,2,1,1,512,512]{5,4,0,3,2,1:T(8,128)(2,1)}, bf16[3,2,1,1,512,512]{5,4,0,3,2,1:T(8,128)(2,1)}, u32[]{:S(2)}, u32[]{:S(2)}) %collective-permute-start.6) | collective-permute-done | bytes 3145760 | tf_op jit(solution)/shard_map/ppermute | solution.py:32
  391.2 12.4 %all_gather.26 = bf16[4096]{0:T(1024)(128)(2,1)S(1)} all-gather(bf16[1024]{0:T(1024)(128)(2,1)S(1)} %copy-done.28), channel_id=1, replica_groups=mesh['ctx'=8,'tp'=4] {'tp'}, dimensions={0}, use_global_device_ids=true | all-gather | bytes 10240 | tf_op jit(solution)/shard_map/all_gather | solution.py:308
  413.2 32.2 %all-gather.9.cloned.1.call-done = bf16[256,4096]{1,0:T(8,128)(2,1)} async-done(((bf16[256,1024]{1,0:T(8,128)(2,1)}), bf16[256,4096]{1,0:T(8,128)(2,1)}) %all-gather.9.cloned.1.call-update) | async-done | bytes 2097168 | tf_op jit(solution)/shard_map/all_gather | solution.py:326
  447.5 13.1 %broadcast_select_fusion.1 = (bf16[3,2,2,1,512,512]{5,4,0,3,2,1:T(8,128)(2,1)S(1)}, bf16[3,2,2,1,512,512]{5,4,0,3,2,1:T(8,128)(2,1)S(1)}, bf16[3,2,2,1,512,512]{...) fusion(bf16[3,2,2,1,512,512]{5,4,0,3,2,1:T(8,128)(2,1)} %collective-permute-done.7, pred[]{:T(512)S(6)} %eq.12, ...), kind=kLoop, calls=%fused_computation.6 | loop fusion | flops 18874368 | bytes 50331648 | tf_op jit(solution)/shard_map/jit(_where)/select_n | solution.py:34
  460.6 5.4 pad_maximum_fusion.1
  466.0 31.5 %copy.38 = bf16[3,2,2,2,512,512]{4,3,2,1,5,0:T(2,128)(2,1)} copy(bf16[3,2,2,2,512,512]{5,4,0,3,2,1:T(8,128)(2,1)} %pad_maximum_fusion.1) | data formatting | bytes 25165824 | tf_op jit(solution)/shard_map/concatenate | solution.py:35
  497.5 21.1 %reshape.102 = bf16[3,4096,512]{1,2,0:T(8,128)(2,1)} reshape(bf16[3,2,2,2,512,512]{4,3,2,1,5,0:T(2,128)(2,1)} %copy.38) | data formatting | bytes 25165824 | tf_op jit(solution)/shard_map/reshape | solution.py:36
  518.6 10.5 %pad_maximum_fusion = bf16[3,2,2,2,512,512]{5,4,0,3,2,1:T(8,128)(2,1)} fusion(bf16[3,2,2,1,512,512]{5,4,0,3,2,1:T(8,128)(2,1)} %get-tuple-element.53, bf16[3,2,2,1,512,512]{5,4,0,3,2,1:T(8,128)(2,1)} %get-tuple-element.54), kind=kLoop, calls=%fused_computation | loop fusion | flops 6291456 | bytes 25165824 | tf_op jit(solution)/shard_map/concatenate | solution.py:35
  529.1 31.5 %copy.36 = bf16[3,2,2,2,512,512]{4,3,2,1,5,0:T(2,128)(2,1)} copy(bf16[3,2,2,2,512,512]{5,4,0,3,2,1:T(8,128)(2,1)} %pad_maximum_fusion) | data formatting | bytes 25165824 | tf_op jit(solution)/shard_map/concatenate | solution.py:35
  560.6 21.2 %reshape.100 = bf16[3,4096,512]{1,2,0:T(8,128)(2,1)} reshape(bf16[3,2,2,2,512,512]{4,3,2,1,5,0:T(2,128)(2,1)} %copy.36) | data formatting | bytes 25165824 | tf_op jit(solution)/shard_map/reshape | solution.py:36
  581.9 6.9 %fusion.23 = bf16[3,256,512]{2,1,0:T(8,128)(2,1)S(1)} fusion(bf16[3,4096,512]{1,2,0:T(8,128)(2,1)} %reshape.102, bf16[256,4096]{1,0:T(8,128)(2,1)S(1)} %copy-done.16, f32[256]{0:T(256)S(1)} %add_rsqrt_fusion, f32[4096]{0:T(1024)S(1)} %convert_element_type.163), kind=kOutput, calls=%fused_computation.65 | convolution fusion | flops 3225812992 | bytes 15483904 | tf_op jit(solution)/shard_map/tr,krc->ktc/dot_general | solution.py:331
  595.6 5.1 fusion.21
  604.2 5.2 fusion.19
  609.5 4.3 fusion.18
  613.8 6.3 fusion.17
  629.9 9.6 %modal_ends.1 = f32[128,128]{1,0:T(8,128)S(1)} custom-call(bf16[3,1024,1024]{2,1,0:T(8,128)(2,1)S(1)} %copy-done.3, f32[3,16,128]{2,1,0:T(8,128)S(1)} %reshape.116.xin_ref, f32[72,128]{1,0:T(8,128)S(1)} %reshape.105.w_ref, f32[128,128]{1,0:T(8,128)S(1)} %reshape.106.p_ref, f32[128,128]{1,0:T(8,128)S(1)} %reshape.107.r_ref, ...), custom_call_target="tpu_custom_call" | custom-call | flops 67108864 | bytes 8388608 | tf_op jit(solution)/shard_map/modal_ends/pallas_call | solution.py:249
  639.4 10.5 %all-gather = f32[1024,128]{1,0:T(8,128)S(1)} all-gather(f32[128,128]{1,0:T(8,128)S(1)} %modal_ends.1), channel_id=2, replica_groups=mesh['ctx'=8,'tp'=4] {'ctx'}, dimensions={0}, use_global_device_ids=true | all-gather | bytes 589824 | tf_op jit(solution)/shard_map/all_gather | solution.py:347
  650.1 18.7 %modal_finish.1 = bf16[1024,1024]{1,0:T(8,128)(2,1)} custom-call(bf16[3,1024,1024]{2,1,0:T(8,128)(2,1)S(1)} %copy-done.3, f32[3,16,128]{2,1,0:T(8,128)S(1)} %reshape.116.xin_ref, f32[72,128]{1,0:T(8,128)S(1)} %reshape.105.w_ref, f32[128,128]{1,0:T(8,128)S(1)} %reshape.106.p_ref, f32[128,128]{1,0:T(8,128)S(1)} %reshape.107.r_ref, ...), custom_call_target="tpu_custom_call" | custom-call | flops 67108864 | bytes 8388608 | tf_op jit(solution)/shard_map/modal_finish/pallas_call | solution.py:249
  (149 shorter events, 85.2 us)
Async XLA Ops:
  7.2 11.0 %copy-start.23 = (bf16[1024,128]{1,0:T(8,128)(2,1)S(1)}, bf16[1024,128]{1,0:T(8,128)(2,1)}, u32[]{:S(2)}) copy-start(bf16[1024,128]{1,0:T(8,128)(2,1)} %param.13) | copy-start | bytes 786436
  7.2 61.4 %all-gather.7.cloned.1.call-start = ((), (), s32[]{:S(2)}) async-start(), calls=%async_computation.4 | async-start | bytes 9437184 | tf_op jit(solution)/shard_map/all_gather | solution.py:301
  7.9 10.4 %copy-start.24 = (f32[3,3,1024]{2,1,0:T(4,128)S(1)}, f32[3,3,1024]{2,1,0:T(4,128)}, u32[]{:S(2)}) copy-start(f32[3,3,1024]{2,1,0:T(4,128)} %param.12) | copy-start | bytes 110596
  7.9 130.4 %reduce-scatter.5.cloned.1.call-start = ((), (), s32[]{:S(2)}) async-start(), calls=%async_computation.5 | async-start | bytes 2621440 | tf_op jit(solution)/shard_map/reduce_scatter | solution.py:322
  10.5 8.5 %collective-permute-start.1 = (bf16[128,1024]{1,0:T(8,128)(2,1)S(1)}, bf16[128,1024]{1,0:T(8,128)(2,1)S(1)}, u32[]{:S(2)}, u32[]{:S(2)}) collective-permute-start(bf16[128,1024]{1,0:T(8,128)(2,1)S(1)} %fusion.35), channel_id=1, source_target_pairs={{0,4},{4,8},{8,12},{12,16},{16,20},{20,24},{24,28},{1,5},{5,9},{9,... | collective-permute-start | bytes 786440 | tf_op jit(solution)/shard_map/ppermute | solution.py:20
  13.7 5.3 collective-permute-start
  75.7 90.2 %reduce-scatter.7.cloned.1.call-start = ((), (), s32[]{:S(2)}) async-start(), calls=%async_computation.6 | async-start | bytes 2621440 | tf_op jit(solution)/shard_map/reduce_scatter | solution.py:322
  97.1 114.2 %reduce-scatter.11.cloned.1.call-start = ((), (), s32[]{:S(2)}) async-start(), calls=%async_computation.8 | async-start | bytes 2621440 | tf_op jit(solution)/shard_map/reduce_scatter | solution.py:322
  130.7 126.0 %reduce-scatter.9.cloned.1.call-start = ((), (), s32[]{:S(2)}) async-start(), calls=%async_computation.7 | async-start | bytes 2621440 | tf_op jit(solution)/shard_map/reduce_scatter | solution.py:322
  138.2 122.9 %copy-start.15 = (bf16[3,512,1024]{2,1,0:T(8,128)(2,1)S(1)}, bf16[3,512,1024]{2,1,0:T(8,128)(2,1)}, u32[]{:S(2)}) copy-start(bf16[3,512,1024]{2,1,0:T(8,128)(2,1)} %param.17) | copy-start | bytes 9437188
  138.2 268.6 %all-gather.15.cloned.1.call-start = ((), (), s32[]{:S(2)}) async-start(), calls=%async_computation.12 | async-start | bytes 2621440 | tf_op jit(solution)/shard_map/all_gather | solution.py:326
  261.0 148.0 %all-gather.13.cloned.1.call-start = ((), (), s32[]{:S(2)}) async-start(), calls=%async_computation.11 | async-start | bytes 2621440 | tf_op jit(solution)/shard_map/all_gather | solution.py:326
  263.0 36.2 %collective-permute-start.2 = (bf16[3,1,1,1,512,512]{5,4,0,3,2,1:T(8,128)(2,1)}, bf16[3,1,1,1,512,512]{5,4,0,3,2,1:T(8,128)(2,1)S(1)}, u32[]{:S(2)}, u32[]{:S(2)}) collective-permute-start(bf16[3,1,1,1,512,512]{5,4,0,3,2,1:T(8,128)(2,1)} %get-tuple-element.40), channel_id=1, source_target_pairs={{0,8},{4,12},{8,0},{12,4},{16,24},{20,28},{24,16},{28,20},{1,9},{5... | collective-permute-start | bytes 4718600 | tf_op jit(solution)/shard_map/ppermute | solution.py:32
  264.5 36.0 %collective-permute-start.5 = (bf16[3,1,1,1,512,512]{5,4,0,3,2,1:T(8,128)(2,1)}, bf16[3,1,1,1,512,512]{5,4,0,3,2,1:T(8,128)(2,1)}, u32[]{:S(2)}, u32[]{:S(2)}) collective-permute-start(bf16[3,1,1,1,512,512]{5,4,0,3,2,1:T(8,128)(2,1)} %get-tuple-element.41), channel_id=1, source_target_pairs={{0,16},{4,20},{8,24},{12,28},{16,0},{20,4},{24,8},{28,12},{1,17},{... | collective-permute-start | bytes 4718600 | tf_op jit(solution)/shard_map/ppermute | solution.py:32
  303.8 7.0 %copy-start.8 = (bf16[3,1,1,1,512,512]{5,4,0,3,2,1:T(8,128)(2,1)}, bf16[3,1,1,1,512,512]{5,4,0,3,2,1:T(8,128)(2,1)S(1)}, u32[]{:S(2)}) copy-start(bf16[3,1,1,1,512,512]{5,4,0,3,2,1:T(8,128)(2,1)S(1)} %get-tuple-element.34) | copy-start | bytes 4718596
  303.8 7.0 %copy-start.10 = (bf16[3,1,1,1,512,512]{5,4,0,3,2,1:T(8,128)(2,1)}, bf16[3,1,1,1,512,512]{5,4,0,3,2,1:T(8,128)(2,1)S(1)}, u32[]{:S(2)}) copy-start(bf16[3,1,1,1,512,512]{5,4,0,3,2,1:T(8,128)(2,1)S(1)} %get-tuple-element.35) | copy-start | bytes 4718596
  307.4 103.8 %all-gather.11.cloned.1.call-start = ((), (), s32[]{:S(2)}) async-start(), calls=%async_computation.10 | async-start | bytes 2621440 | tf_op jit(solution)/shard_map/all_gather | solution.py:326
  307.4 69.1 %collective-permute-start.6 = (bf16[3,2,1,1,512,512]{5,4,0,3,2,1:T(8,128)(2,1)}, bf16[3,2,1,1,512,512]{5,4,0,3,2,1:T(8,128)(2,1)}, u32[]{:S(2)}, u32[]{:S(2)}) collective-permute-start(bf16[3,2,1,1,512,512]{5,4,0,3,2,1:T(8,128)(2,1)} %pad_maximum_fusion.5), channel_id=1, source_target_pairs={{0,8},{4,12},{8,0},{12,4},{16,24},{20,28},{24,16},{28,20},{1,9},{5... | collective-permute-start | bytes 9437192 | tf_op jit(solution)/shard_map/ppermute | solution.py:32
  310.7 73.2 %collective-permute-start.3 = (bf16[3,1,2,1,512,512]{5,4,0,3,2,1:T(8,128)(2,1)}, bf16[3,1,2,1,512,512]{5,4,0,3,2,1:T(8,128)(2,1)}, u32[]{:S(2)}, u32[]{:S(2)}) collective-permute-start(bf16[3,1,2,1,512,512]{5,4,0,3,2,1:T(8,128)(2,1)} %pad_maximum_fusion.4), channel_id=1, source_target_pairs={{0,16},{4,20},{8,24},{12,28},{16,0},{20,4},{24,8},{28,12},{1,17},{... | collective-permute-start | bytes 9437192 | tf_op jit(solution)/shard_map/ppermute | solution.py:32
  312.2 133.2 %all-gather.9.cloned.1.call-start = ((), (), s32[]{:S(2)}) async-start(), calls=%async_computation.9 | async-start | bytes 2621440 | tf_op jit(solution)/shard_map/all_gather | solution.py:326
  383.9 63.6 %collective-permute-start.7 = (bf16[3,2,2,1,512,512]{5,4,0,3,2,1:T(8,128)(2,1)}, bf16[3,2,2,1,512,512]{5,4,0,3,2,1:T(8,128)(2,1)}, u32[]{:S(2)}, u32[]{:S(2)}) collective-permute-start(bf16[3,2,2,1,512,512]{5,4,0,3,2,1:T(8,128)(2,1)} %pad_maximum_fusion.3), channel_id=1, source_target_pairs={{0,4},{4,0},{8,12},{12,8},{16,20},{20,16},{24,28},{28,24},{1,5},{5... | collective-permute-start | bytes 18874376 | tf_op jit(solution)/shard_map/ppermute | solution.py:32
  386.1 17.5 %copy-start.27 = (f32[3,3,1024]{2,1,0:T(4,128)S(1)}, f32[3,3,1024]{2,1,0:T(4,128)}, u32[]{:S(2)}) copy-start(f32[3,3,1024]{2,1,0:T(4,128)} %param.18) | copy-start | bytes 110596
  386.1 17.5 %copy-start.25 = (f32[16,1024]{1,0:T(8,128)S(1)}, f32[16,1024]{1,0:T(8,128)}, u32[]{:S(2)}) copy-start(f32[16,1024]{1,0:T(8,128)} %param.19) | copy-start | bytes 196612
  386.1 17.6 %copy-start.26 = (f32[16,1024]{1,0:T(8,128)S(1)}, f32[16,1024]{1,0:T(8,128)}, u32[]{:S(2)}) copy-start(f32[16,1024]{1,0:T(8,128)} %param.20) | copy-start | bytes 196612
  390.6 56.9 %collective-permute-start.4 = (bf16[3,2,2,1,512,512]{5,4,0,3,2,1:T(8,128)(2,1)}, bf16[3,2,2,1,512,512]{5,4,0,3,2,1:T(8,128)(2,1)}, u32[]{:S(2)}, u32[]{:S(2)}) collective-permute-start(bf16[3,2,2,1,512,512]{5,4,0,3,2,1:T(8,128)(2,1)} %pad_maximum_fusion.2), channel_id=1, source_target_pairs={{0,4},{4,0},{8,12},{12,8},{16,20},{20,16},{24,28},{28,24},{1,5},{5... | collective-permute-start | bytes 18874376 | tf_op jit(solution)/shard_map/ppermute | solution.py:32
  560.6 21.2 %copy-start.16 = (bf16[256,4096]{1,0:T(8,128)(2,1)S(1)}, bf16[256,4096]{1,0:T(8,128)(2,1)}, u32[]{:S(2)}) copy-start(bf16[256,4096]{1,0:T(8,128)(2,1)} %all-gather.15.cloned.1.call-done) | copy-start | bytes 6291460
  581.8 8.2 %copy-start.14 = (bf16[3,4096,512]{1,2,0:T(8,128)(2,1)S(1)}, bf16[3,4096,512]{1,2,0:T(8,128)(2,1)}, u32[]{:S(2)}) copy-start(bf16[3,4096,512]{1,2,0:T(8,128)(2,1)} %reshape.100) | copy-start | bytes 37748740
  581.8 13.7 %slice-start = ((s8[12582912]{0:T(1024)(128)(4,1)}), s8[4194304]{0:T(1024)(128)(4,1)S(1)}, s32[]{:S(2)}) async-start(s8[12582912]{0:T(1024)(128)(4,1)} %bitcast.79), calls=%async_computation.13 | async-start | bytes 8388608
  581.9 13.7 %slice-start.1 = ((s8[12582912]{0:T(1024)(128)(4,1)}), s8[4194304]{0:T(1024)(128)(4,1)S(1)}, s32[]{:S(2)}) async-start(s8[12582912]{0:T(1024)(128)(4,1)} %bitcast.79), calls=%async_computation.14 | async-start | bytes 8388608
  593.5 7.1 %copy-start.17 = (bf16[256,4096]{1,0:T(8,128)(2,1)S(1)}, bf16[256,4096]{1,0:T(8,128)(2,1)}, u32[]{:S(2)}) copy-start(bf16[256,4096]{1,0:T(8,128)(2,1)} %all-gather.13.cloned.1.call-done) | copy-start | bytes 6291460
  593.6 33.5 %collective-permute-start.8 = (bf16[3,2,1024]{2,1,0:T(2,128)(2,1)S(1)}, bf16[3,2,1024]{2,1,0:T(2,128)(2,1)S(1)}, u32[]{:S(2)}, u32[]{:S(2)}) collective-permute-start(bf16[3,2,1024]{2,1,0:T(2,128)(2,1)S(1)} %pad_maximum_fusion.7), channel_id=1, source_target_pairs={{0,4},{4,8},{8,12},{12,16},{16,20},{20,24},{24,28},{1,5},{5,9},{9,... | collective-permute-start | bytes 36872 | tf_op jit(solution)/shard_map/ppermute | solution.py:20
  613.8 6.4 copy-start.19
  (18 other events, 65.0 us)
Sparse Core Ops, SparseCore 0:
  9.9 58.6 all-gather.6
  75.8 43.8 reduce-scatter.4
  122.7 43.1 reduce-scatter.6
  168.0 43.1 reduce-scatter.10
  213.5 43.1 reduce-scatter.8
  261.1 45.2 all-gather.14
  308.0 44.8 all-gather.12
  354.4 44.6 all-gather.10
  400.7 44.6 all-gather.8
